TPU v7x, 128 devices: a whole 4x4x4 slice. The times are simulated.
128 devices in a mesh: grp: 4 (over y_lo, core), ep: 32 (over x, y_hi, z).
Axes of the slice: x: 4, y: 4 (y_hi: 2, y_lo: 2; y = y_hi * 2 + y_lo), z: 4, core: 2. Of those that a mesh axis runs over, the one named last changes fastest.
Arguments:
- cotangent: bfloat16 [16384, 3584], P(('grp', 'ep')), may hold values from -4 to 4
- routes: int32 [16384, 4], P(('grp', 'ep')), may hold values from 0 to 31, as said below
- gates: float32 [16384, 4], P(('grp', 'ep')), may hold values from 0.05 to 1
- pre_act: bfloat16 [16384, 4, 2048], P(('grp', 'ep')), may hold values from -6 to 6
- down_weight: bfloat16 [32, 1024, 3584], P('ep'), may hold values from -0.1875 to 0.1875
Outputs:
- pre_grad: bfloat16 [16384, 4, 2048], P(('grp', 'ep'))
- weight_grad: bfloat16 [32, 1024, 3584], P('ep', 'grp')
Inputs may be any that keep to these rules, and one draw needn't show every extreme that they name: `routes`: each row names 4 different experts. In every block of 128 rows one expert, the same in all blocks, is named exactly 96 times; one other expert, the same in all blocks, exactly 20 times; every remaining expert 1 to 20 times.
All inputs are finite; a program needn't handle non-finite values.
Results may differ from a plain program's by a relative error of at most 0.025.
Values may be sent and summed in bfloat16 or wider, within the bound.
A program may use at most 128 MiB of HBM per device.

v0:
```python
import jax
import jax.numpy as jnp
from jax import lax
from jax.sharding import PartitionSpec as P


def from_root(value, axis, source):
    kept = jnp.where(lax.axis_index(axis) == source, value, 0).astype(value.dtype)
    return lax.psum(kept, axis)


def swish_terms(pre_rows, hidden):
    gate_pre = pre_rows[:, :hidden].astype(jnp.float32)
    up_pre = pre_rows[:, hidden:].astype(jnp.float32)
    return (gate_pre, up_pre, jax.nn.sigmoid(gate_pre))


def compact(selected, out_width):
    position = jnp.cumsum(selected.astype(jnp.int32)) - 1
    target = jnp.where(selected, position, out_width)
    source = jnp.arange(selected.shape[0], dtype=jnp.int32)
    filled = (
        jnp.full((out_width,), selected.shape[0], jnp.int32).at[target].set(source, mode="drop")
    )
    return (filled, position)


def local(cotangent, routes, gates, pre_act, down_weight):
    tokens, top_count = routes.shape
    hidden = down_weight.shape[1]
    features = down_weight.shape[2]
    ep_size = lax.axis_size("ep")
    my_index = lax.axis_index("ep")
    slot_count = tokens * top_count
    hot_rows = 3 * tokens // 4
    capacity = 3 * (slot_count - hot_rows) // (2 * (ep_size - 1))
    flat_routes = routes.reshape(slot_count)
    expert_ids = jnp.arange(ep_size, dtype=jnp.int32)
    onehot = (flat_routes[:, None] == expert_ids[None, :]).astype(jnp.int32)
    hot_expert = jnp.argmax(jnp.sum(onehot, axis=0))
    bucket_rank = jnp.sum((jnp.cumsum(onehot, axis=0) - onehot) * onehot, axis=1)
    is_hot = flat_routes == hot_expert
    gate_pre, up_pre, sigmoid_gate = swish_terms(pre_act.reshape(slot_count, 2 * hidden), hidden)
    activation = (gate_pre * sigmoid_gate * up_pre).astype(jnp.bfloat16)
    scaled = (
        (gates[:, :, None] * cotangent.astype(jnp.float32)[:, None, :])
        .astype(jnp.bfloat16)
        .reshape(slot_count, features)
    )
    cold_target = jnp.where(is_hot, ep_size * capacity, flat_routes * capacity + bucket_rank)
    cold_source = (
        jnp.full((ep_size * capacity,), slot_count, jnp.int32)
        .at[cold_target]
        .set(jnp.arange(slot_count, dtype=jnp.int32), mode="drop")
    )
    send_grad = jnp.take(scaled, cold_source, axis=0, mode="fill", fill_value=0).reshape(
        ep_size, capacity, features
    )
    send_act = jnp.take(activation, cold_source, axis=0, mode="fill", fill_value=0).reshape(
        ep_size, capacity, hidden
    )
    received_grad, received_act = (
        lax.all_to_all(send_grad, "ep", split_axis=0, concat_axis=0, tiled=True),
        lax.all_to_all(send_act, "ep", split_axis=0, concat_axis=0, tiled=True),
    )
    received_grad = received_grad.reshape(ep_size * capacity, features)
    received_act = received_act.reshape(ep_size * capacity, hidden)
    own_weight = down_weight[0]
    owner_grad = jnp.dot(received_grad, own_weight.T, preferred_element_type=jnp.float32).astype(
        jnp.bfloat16
    )
    returned = lax.all_to_all(
        owner_grad.reshape(ep_size, capacity, hidden), "ep", split_axis=0, concat_axis=0, tiled=True
    )
    hot_weight = from_root(own_weight, "ep", hot_expert)
    hot_source, hot_position = compact(is_hot, hot_rows)
    hot_grad = jnp.take(scaled, hot_source, axis=0, mode="fill", fill_value=0)
    hot_act = jnp.take(activation, hot_source, axis=0, mode="fill", fill_value=0)
    hot_hidden = jnp.dot(hot_grad, hot_weight.T, preferred_element_type=jnp.float32).astype(
        jnp.bfloat16
    )
    shadow_part = jnp.dot(hot_act.T, hot_grad, preferred_element_type=jnp.float32).astype(
        jnp.bfloat16
    )
    cold_back_rows = jnp.take(
        returned.reshape(ep_size * capacity, hidden), cold_target, axis=0, mode="fill", fill_value=0
    )
    hot_back_rows = jnp.take(
        hot_hidden, jnp.where(is_hot, hot_position, hot_rows), axis=0, mode="fill", fill_value=0
    )
    hidden_grad = jnp.where(is_hot[:, None], hot_back_rows, cold_back_rows).astype(jnp.float32)
    gate_part = hidden_grad * up_pre * sigmoid_gate * (1.0 + gate_pre * (1.0 - sigmoid_gate))
    up_part = hidden_grad * gate_pre * sigmoid_gate
    pre_grad = (
        jnp.concatenate([gate_part, up_part], axis=1)
        .astype(jnp.bfloat16)
        .reshape(tokens, top_count, 2 * hidden)
    )
    owner_flag = my_index == hot_expert
    shadow_total = lax.psum(shadow_part, "ep").astype(jnp.float32)
    summed = lax.psum_scatter(
        (
            jnp.dot(received_act.T, received_grad, preferred_element_type=jnp.float32)
            + jnp.where(owner_flag, shadow_total, 0.0)
        ).astype(jnp.bfloat16),
        "grp",
        scatter_dimension=0,
        tiled=True,
    )
    return (pre_grad, summed[None])


def solution(mesh):
    in_specs = (
        P(("grp", "ep"), None),
        P(("grp", "ep"), None),
        P(("grp", "ep"), None),
        P(("grp", "ep"), None, None),
        P("ep", None, None),
    )
    out_specs = (P(("grp", "ep"), None, None), P("ep", "grp", None))
    return jax.shard_map(local, mesh=mesh, in_specs=in_specs, out_specs=out_specs, check_vma=False)
```

profile of v0, /device:TPU:1, one launch (start us, length us, event | category | flops | bytes accessed | tf_op | source)
XLA Modules:
  0.0 654.9 jit_solution(16711487107766020369)
XLA Ops:
  7.2 0.0 all-reduce.3.cloned.1.call-start
  7.2 0.8 copy.18
  8.0 0.1 reshape.191
  8.1 0.1 reshape.190
  8.2 1.2 reduce-window.19
  9.4 0.2 slice_reduce_fusion
  9.7 0.2 fusion.20
  9.8 0.7 iota_reduce_fusion
  10.5 0.6 compare_convert_fusion
  11.1 1.3 broadcast_compare_fusion
  12.5 0.7 broadcast_multiply_fusion
  13.1 0.3 reduce-window.15
  13.5 0.1 slice.19
  13.6 0.1 slice_reduce_fusion.1
  13.7 0.7 compare_and_fusion.3
  14.4 0.1 copy.20
  14.5 0.1 eq.72
  14.7 0.1 copy.23
  14.8 0.1 mul.77
  14.9 2.4 scatter_custom_fusion
  17.4 5.2 mul.69
  22.6 9.0 %mul.70 = f32[512,3584]{1,0:T(8,128)} reshape(f32[128,4,3584]{2,1,0:T(4,128)} %mul.69) | data formatting | bytes 14680064 | tf_op jit(solution)/shard_map/mul | solution.py:46
  31.6 0.0 copy-done.2
  31.6 0.1 copy.21
  31.7 0.1 mul.67
  31.8 2.5 reshape.197
  34.3 0.7 fusion.6
  35.0 5.9 multiply_convert_fusion
  40.9 5.0 gather_fusion
  46.0 0.8 gather_fusion.5
  47.4 6.6 %bitcast_select_fusion = bf16[1024,3584]{1,0:T(8,128)(2,1)} fusion(bf16[1,1024,3584]{2,1,0:T(8,128)(2,1)} %param.9, pred[]{:T(512)S(6)} %eq.73), kind=kLoop, calls=%fused_computation.13 | loop fusion | flops 3670016 | bytes 14680065 | tf_op jit(solution)/shard_map/jit(_where)/select_n | solution.py:8
  54.0 5.1 convolution_convert_fusion
  59.1 0.0 all-reduce.3.cloned.1.call-update
  59.2 2.6 scatter_custom_fusion.1
  61.8 0.1 broadcast_in_dim.122
  61.9 3.5 gather_fusion.4
  65.4 3.2 gather.34
  68.6 2.7 broadcast_select_fusion.1
  71.3 11.7 %all-to-all-start.2 = ((bf16[32,20,1024]{2,1,0:T(8,128)(2,1)}), bf16[32,20,1024]{2,1,0:T(8,128)(2,1)}, u32[]{:S(2)}, u32[]{:S(2)}) async-start(bf16[32,20,1024]{2,1,0:T(8,128)(2,1)} %broadcast_select_fusion.1), calls=%async_computation.2 | async-start | bytes 3145728 | tf_op jit(solution)/shard_map/all_to_all | solution.py:64
  83.1 0.0 reduce-scatter.2.cloned.1.call-start
  83.1 13.2 %gather_fusion.2 = bf16[640,3584]{1,0:T(8,128)(2,1)} fusion(bf16[512,3584]{1,0:T(8,128)(2,1)} %multiply_convert_fusion, s32[1024]{0:T(1024)S(1)} %pad_clamp_fusion.1), kind=kCustom, calls=%fused_computation.2 | custom fusion | bytes 9177600 | tf_op jit(solution)/shard_map/jit(_take)/gather | solution.py:56
  96.3 7.2 %gather.31 = bf16[32,20,3584]{2,1,0:T(8,128)(2,1)} reshape(bf16[640,3584]{1,0:T(8,128)(2,1)} %gather_fusion.2) | data formatting | bytes 9175040 | tf_op jit(solution)/shard_map/jit(_take)/gather | solution.py:56
  103.6 5.4 broadcast_select_fusion
  109.0 8.4 %all-to-all-done.2 = bf16[32,20,1024]{2,1,0:T(8,128)(2,1)} async-done(((bf16[32,20,1024]{2,1,0:T(8,128)(2,1)}), bf16[32,20,1024]{2,1,0:T(8,128)(2,1)}, u32[]{:S(2)}, u32[]{:S(2)}) %all-to-all-start.2) | async-done | bytes 1310752 | tf_op jit(solution)/shard_map/all_to_all | solution.py:64
  117.4 111.3 %all_to_all.15 = bf16[32,20,3584]{2,1,0:T(8,128)(2,1)} all-to-all(bf16[32,20,3584]{2,1,0:T(8,128)(2,1)} %broadcast_select_fusion), channel_id=1, replica_groups=mesh['grp'=4,'ep'=32] {'ep'}, dimensions={0} | all-to-all | bytes 9175040 | tf_op jit(solution)/shard_map/all_to_all | solution.py:63
  228.7 305.0 %all-reduce.3.cloned.1.call-done = (bf16[1024,3584]{1,0:T(8,128)(2,1)}, bf16[1024,3584]{1,0:T(8,128)(2,1)}) async-done(((bf16[1024,3584]{1,0:T(8,128)(2,1)}, bf16[1024,3584]{1,0:T(8,128)(2,1)}), (bf16[1024,3584]{1,0:T(8,128)(2,1)}, bf16[1024,3584]{1,0:T(8,128)(2,1)})) %all-reduce.3.cloned.1.call-update) | async-done | bytes 14680080 | tf_op jit(solution)/shard_map/psum | solution.py:9
  533.8 11.6 %fusion = bf16[1024,3584]{1,0:T(8,128)(2,1)} fusion(bf16[1024,3584]{1,0:T(8,128)(2,1)} %get-tuple-element.7, bf16[32,20,1024]{2,1,0:T(8,128)(2,1)} %all-to-all-done.2, bf16[32,20,3584]{2,1,0:T(8,128)(2,1)} %all_to_all.15, pred[]{:T(512)S(6)} %eq.73), kind=kOutput, calls=%fused_computation.9 | convolution fusion | flops 4712300544 | bytes 20578304 | tf_op jit(solution)/shard_map/dot_general | solution.py:103
  545.4 0.0 reduce-scatter.2.cloned.1.call-update
  545.4 7.3 %reshape.194 = bf16[640,3584]{1,0:T(8,128)(2,1)} reshape(bf16[32,20,3584]{2,1,0:T(8,128)(2,1)} %all_to_all.15) | data formatting | bytes 9175040 | tf_op jit(solution)/shard_map/reshape | solution.py:66
  552.7 9.4 %fusion.13 = bf16[640,1024]{1,0:T(8,128)(2,1)S(1)} fusion(bf16[640,3584]{1,0:T(8,128)(2,1)} %reshape.194, bf16[1,1024,3584]{2,1,0:T(8,128)(2,1)} %param.9), kind=kOutput, calls=%fused_computation.33 | convolution fusion | flops 4698275840 | bytes 13238272 | tf_op jit(solution)/shard_map/dot_general | solution.py:69
  562.1 1.3 reshape.195
  563.4 6.8 %all-to-all-start.1 = ((bf16[32,20,1024]{2,1,0:T(8,128)(2,1)}), bf16[32,20,1024]{2,1,0:T(8,128)(2,1)}, u32[]{:S(2)}, u32[]{:S(2)}) async-start(bf16[32,20,1024]{2,1,0:T(8,128)(2,1)} %reshape.195), calls=%async_computation.1 | async-start | bytes 3145728 | tf_op jit(solution)/shard_map/all_to_all | solution.py:72
  570.2 18.7 %all-to-all-done.1 = bf16[32,20,1024]{2,1,0:T(8,128)(2,1)} async-done(((bf16[32,20,1024]{2,1,0:T(8,128)(2,1)}), bf16[32,20,1024]{2,1,0:T(8,128)(2,1)}, u32[]{:S(2)}, u32[]{:S(2)}) %all-to-all-start.1) | async-done | bytes 1310752 | tf_op jit(solution)/shard_map/all_to_all | solution.py:72
  588.9 2.3 reshape.196
  591.2 2.8 gather_fusion.3
  594.0 5.7 convolution_convert_fusion.1
  599.7 0.0 copy-start.1
  599.7 2.8 gather_fusion.1
  602.5 0.0 copy-done.1
  602.5 3.7 fusion.5
  606.2 1.5 concatenate.10
  607.7 1.5 concatenate.9
  609.1 2.6 pad_maximum_fusion
  611.8 36.3 %reduce-scatter.2.cloned.1.call-done = bf16[256,3584]{1,0:T(8,128)(2,1)} async-done(((bf16[1024,3584]{1,0:T(8,128)(2,1)}), bf16[256,3584]{1,0:T(8,128)(2,1)}) %reduce-scatter.2.cloned.1.call-update) | async-done | bytes 1835024 | tf_op jit(solution)/shard_map/reduce_scatter | solution.py:101
  (19 shorter events, 0.2 us)
Async XLA Ops:
  7.2 526.6 %all-reduce.3.cloned.1.call-start = ((), (), s32[]{:S(2)}) async-start(), calls=%async_computation.5 | async-start | bytes 29360128 | tf_op jit(solution)/shard_map/psum | solution.py:9
  22.6 9.0 %copy-start.2 = (f32[128,4]{0,1:T(4,128)S(1)}, f32[128,4]{0,1:T(4,128)}, u32[]{:S(2)}) copy-start(f32[128,4]{0,1:T(4,128)} %param.7) | copy-start | bytes 6148
  47.4 6.6 %copy-start = (bf16[96,3584]{1,0:T(8,128)(2,1)S(1)}, bf16[96,3584]{1,0:T(8,128)(2,1)}, u32[]{:S(2)}) copy-start(bf16[96,3584]{1,0:T(8,128)(2,1)} %gather_fusion) | copy-start | bytes 2064388
  71.3 46.1 %all-to-all-start.2 = ((bf16[32,20,1024]{2,1,0:T(8,128)(2,1)}), bf16[32,20,1024]{2,1,0:T(8,128)(2,1)}, u32[]{:S(2)}, u32[]{:S(2)}) async-start(bf16[32,20,1024]{2,1,0:T(8,128)(2,1)} %broadcast_select_fusion.1), calls=%async_computation.2 | async-start | bytes 3145728 | tf_op jit(solution)/shard_map/all_to_all | solution.py:64
  83.1 565.1 %reduce-scatter.2.cloned.1.call-start = ((), (), s32[]{:S(2)}) async-start(), calls=%async_computation.4 | async-start | bytes 9175040 | tf_op jit(solution)/shard_map/reduce_scatter | solution.py:101
  563.4 25.5 %all-to-all-start.1 = ((bf16[32,20,1024]{2,1,0:T(8,128)(2,1)}), bf16[32,20,1024]{2,1,0:T(8,128)(2,1)}, u32[]{:S(2)}, u32[]{:S(2)}) async-start(bf16[32,20,1024]{2,1,0:T(8,128)(2,1)} %reshape.195), calls=%async_computation.1 | async-start | bytes 3145728 | tf_op jit(solution)/shard_map/all_to_all | solution.py:72
  599.7 2.8 copy-start.1
Sparse Core Ops, SparseCore 0:
  59.3 474.4 all-reduce.2
  545.5 102.5 reduce-scatter.1
where the time goes:
time: 656 us; the launch traced here: 655 us
  waiting for transfers between devices  369 us (56%)
  blocking collectives  111 us (17%)
  local copies, waits for them, and re-layouts  76.3 us (12%)
  other arithmetic  33.5 us (5%)
  matrix products  31.8 us (5%)
  starting transfers between devices  18.6 us (3%)
  between operations  14.9 us (2%)
    psum x1, waiting for transfers between devices, from_root(): return lax.psum(kept, axis)  305 us
    all_to_all x1, blocking collectives, local(): lax.all_to_all(send_grad, 'ep', split_axis=0, concat_axis=0, tiled=True)  111 us
    reduce_scatter x1, waiting for transfers between devices, local(): lax.psum_scatter((jnp.dot(received_act.T, received_grad, preferred_elemen...  36.3 us
    gather x2, local copies, waits for them, and re-layouts, local(): jnp.take(scaled, cold_source, axis=0, mode='fill', fill_value=0)  20.5 us
    all_to_all x1, waiting for transfers between devices, local(): lax.all_to_all(owner_grad.reshape(ep_size, capacity, hidden), 'ep', split...  18.7 us
    mul x3, local copies, waits for them, and re-layouts, local(): gates[:, :, None] * cotangent.astype(jnp.float32)[:, None, :]  14.3 us
  transfers between devices with their start and end apart: 4, of which 4 were waited for; matrix products, arithmetic and copies ran while one was open for 12% of the time, Pallas kernels for 0%

commit v1 on v0

v1 whole, which is shorter than its diff:
```python
import functools

import jax
import jax.numpy as jnp
from jax import lax
from jax.experimental import pallas as pl
from jax.experimental.pallas import tpu as pltpu
from jax.sharding import PartitionSpec as P

MESH = pl.DeviceIdType.MESH
BF = jnp.bfloat16
F32 = jnp.float32

TOK = 128
TOPK = 4
SLOT = TOK * TOPK
HID = 1024
D = 3584
CAP = 20
NX, NZ = 4, 4
NJ = 8
NQ = 4
DQ = D // NQ
ROW = NX * CAP
COLD = NJ * ROW
HALF = D // 2


def dot(a, b, dims=((1,), (0,))):
    return lax.dot_general(a, b, (dims, ((), ())), preferred_element_type=F32)


NN = ((1,), (0,))
NT = ((1,), (1,))
TN = ((0,), (0,))


def iota(shape, dim):
    return lax.broadcasted_iota(jnp.int32, shape, dim)


def onehot(flag):
    return flag.astype(F32).astype(BF)


def main_kernel(
    cot, meta, rnat, pre, w,
    hid, wg,
    cg, ch, mg, pa, wq,
    ohx, ohg, pm, gc, gh,
    acts, actx, actp, actr,
    s, sr, hacc, hgx, ret,
    wgs, cr, ys, yr,
    a1r, a2s, a2r, a3s, a3r, ags, wh,
    aht, at, hht, hhs, hhacc, sh, hp, rsb, gp, g1, g2, g3,
    ssem, rsem, lsem,
):
    g, e = lax.axis_index("grp"), lax.axis_index("ep")
    yl, c = g // 2, g % 2
    x, yh, z = e // 8, (e // 4) % 2, e % 4

    def dev(dx=0, dyh=0, dz=0, dyl=0, dc=0):
        return (
            ((yl + dyl) % 2) * 2 + (c + dc) % 2,
            (((x + dx) % 4) * 2 + (yh + dyh) % 2) * 4 + (z + dz) % 4,
        )

    counts = [0, 0]

    def remote(src, dst, **to):
        k = counts[0]
        counts[0] += 1
        cp = pltpu.make_async_remote_copy(
            src_ref=src, dst_ref=dst, send_sem=ssem.at[k], recv_sem=rsem.at[k],
            device_id=dev(**to), device_id_type=MESH,
        )
        cp.start()
        return cp

    def here(src, dst):
        k = counts[1]
        counts[1] += 1
        cp = pltpu.make_async_copy(src, dst, lsem.at[k])
        cp.start()
        return cp

    sent = []

    def arrived(copies):
        for cp in copies:
            cp.wait_recv()
        sent.extend(copies)

    def left(copies):
        gone = [id(cp) for cp in copies]
        sent[:] = [cp for cp in sent if id(cp) not in gone]
        for cp in copies:
            cp.wait_send()

    def cols(q):
        return pl.ds(q * DQ, DQ)

    peers = [dict(dx=d) for d in range(1, 4)] + [dict(dx=d, dc=1) for d in range(4)]
    peers += [
        dict(dyh=a, dyl=b, dz=d)
        for a in range(2) for b in range(2) for d in range(4) if a or b or d
    ]
    barrier = pltpu.get_barrier_semaphore()
    for to in peers:
        pl.semaphore_signal(barrier, inc=1, device_id=dev(**to), device_id_type=MESH)
    own_cot = [here(cot.at[:, cols(q)], cg.at[q, pl.ds(x * TOK, TOK)]) for q in range(NQ)]
    pa_copy = here(pre, pa)
    pl.semaphore_wait(barrier, len(peers))

    meta_cp = [remote(meta, mg.at[x], dx=d) for d in range(1, 4)]
    meta_cp += [remote(meta, mg.at[4 + x], dx=d, dc=1) for d in range(4)]
    cot_cp = []
    for q in range(NQ):
        cot_cp.append([
            remote(cot.at[:, cols(q)], cg.at[q, pl.ds(x * TOK, TOK)], dx=d) for d in (1, 3, 2)
        ])
    base = 512 * yl + 256 * c
    a1_cp = []
    for d in range(1, 4):
        zt = (z + d) % 4
        for xt in range(NX):
            a1_cp.append(remote(w.at[pl.ds(base + 64 * xt + 16 * zt, 16)], a1r.at[z, xt], dz=d))
    a1_own = [
        here(w.at[pl.ds(base + 64 * xt + 16 * z, 16)], a1r.at[z, xt]) for xt in range(NX)
    ]
    w_copy = [here(w.at[:, cols(q)], wq.at[q]) for q in range(NQ)]
    mg[x] = meta[...]

    rn = rnat[...]
    eid = iota((32, SLOT), 0).astype(F32)
    member = (rn == eid).astype(F32)
    tri = onehot(iota((SLOT, SLOT), 0) < iota((SLOT, SLOT), 1))
    rank = dot(member.astype(BF), tri)
    hotv = (jnp.sum(member, axis=1, keepdims=True) >= 64.0).astype(F32)
    token = lax.shift_right_logical(iota((32, SLOT), 1), 2).astype(F32)
    place = (1.0 - hotv) * (eid * CAP + rank) + hotv * (COLD + token)
    key = jnp.sum(member * place, axis=0, keepdims=True)
    for i in range((COLD + TOK) // 128):
        ohx[pl.ds(i * 128, 128), :] = onehot(iota((128, SLOT), 0).astype(F32) + i * 128.0 == key)
    e1 = iota((32, 1), 0)

    def hot_is(flag):
        return jnp.sum(hotv * flag.astype(F32), axis=0, keepdims=True)

    hotid = jnp.sum(hotv * e1.astype(F32), axis=0, keepdims=True)
    hot_x = [hot_is(lax.shift_right_logical(e1, 3) == k) for k in range(4)]
    hot_z = [hot_is((e1 & 3) == k) for k in range(4)]
    hot_y = [hot_is((lax.shift_right_logical(e1, 2) & 1) == k) for k in range(2)]

    pa_copy.wait()

    def act_step(i, carry):
        rows = pa[pl.ds(i * 8, 8)].reshape(32, 2 * HID).astype(F32)
        gate, up = rows[:, :HID], rows[:, HID:]
        hid[pl.ds(pl.multiple_of(i * 32, 32), 32), :] = (
            gate * jax.nn.sigmoid(gate) * up
        ).astype(BF)
        return carry

    lax.fori_loop(0, TOK // 8, act_step, 0)

    def acts_step(i, carry):
        r = pl.ds(pl.multiple_of(i * 256, 256), 256)
        acts[r, :] = dot(ohx[r, :], hid[...]).astype(BF)
        return carry

    lax.fori_loop(0, 3, acts_step, 0)
    actx_cp = [
        remote(acts.at[pl.ds(((x + d) % 4) * 160, 160)], actx.at[pl.ds(x * 160, 160)], dx=d)
        for d in (1, 3, 2)
    ]
    actx_own = here(acts.at[pl.ds(x * 160, 160)], actx.at[pl.ds(x * 160, 160)])
    eye = onehot(iota((TOK, TOK), 0) == iota((TOK, TOK), 1))
    aht[...] = dot(acts[pl.ds(COLD, TOK), :], eye, TN).astype(BF)
    at_cp, at_own = [], []
    for cc in range(2):
        for d in range(4):
            for h in range(2):
                src = aht.at[pl.ds(512 * h + 256 * ((c + cc) % 2) + 64 * ((x + d) % 4), 64)]
                dst = at.at[pl.ds(64 * h, 64), pl.ds((cc * 4 + x) * TOK, TOK)]
                if cc or d:
                    at_cp.append(remote(src, dst, dx=d, dc=cc))
                else:
                    at_own.append(here(src, dst))

    arrived(meta_cp)
    tri1 = onehot(iota((TOK, TOK), 0) < iota((TOK, TOK), 1))
    ej = (iota((NJ, TOK), 0) + 8 * x).astype(F32)
    keys, gates8 = [], []
    for b in range(NX):
        m = mg[b]
        hit = [(m[k:k + 1] == ej) for k in range(TOPK)]
        mem8 = sum(f.astype(F32) for f in hit)
        gates8.append(sum(jnp.where(hit[k], m[4 + k:5 + k], 0.0) for k in range(TOPK)))
        rank8 = dot(mem8.astype(BF), tri1)
        mem8 = mem8 * (ej != hotid).astype(F32)
        keys.append(jnp.where(mem8 > 0, rank8 + CAP * b, -1.0))
    keys = jnp.concatenate(keys, axis=1)
    gates8 = jnp.concatenate(gates8, axis=1)
    rows80 = iota((ROW, SLOT), 0).astype(F32)
    for j in range(NJ):
        flag = rows80 == keys[j:j + 1]
        ohg[pl.ds(j * ROW, ROW), :] = onehot(flag)
        col = jnp.sum(jnp.where(flag, gates8[j:j + 1], 0.0), axis=1, keepdims=True)
        gc[pl.ds(j * ROW, ROW), :] = jnp.broadcast_to(col, (ROW, 128))
    diag = iota((TOK, TOK), 0) == iota((TOK, TOK), 1)
    for b in range(2 * NX):
        m = mg[b]
        row = sum(jnp.where(m[k:k + 1] == hotid, m[4 + k:5 + k], 0.0) for k in range(TOPK))
        col = jnp.sum(jnp.where(diag, row, 0.0), axis=1, keepdims=True)
        gh[pl.ds(b * TOK, TOK), :] = jnp.broadcast_to(col, (TOK, 128))
    o = iota((COLD, 128), 0)
    oj = sum((o >= ROW * k).astype(jnp.int32) for k in range(1, NJ))
    orem = o - ROW * oj
    ob = sum((orem >= CAP * k).astype(jnp.int32) for k in range(1, NX))
    want = ob * 160 + oj * CAP + (orem - CAP * ob)
    for k in range(COLD // 128):
        pm[:, pl.ds(k * 128, 128)] = onehot(want == iota((COLD, 128), 1) + k * 128)

    jme = yh * 4 + z
    zy = [(0, 1), (0, 3), (1, 0), (0, 2), (1, 1), (1, 3), (1, 2)]

    def jat(a, d):
        return ((yh + a) % 2) * 4 + (z + d) % 4

    def spread(src, dst):
        cps = [
            remote(src.at[pl.ds(jat(a, d) * ROW, ROW)], dst.at[pl.ds(jme * ROW, ROW)],
                   dyh=a, dyl=a, dz=d)
            for a, d in zy
        ]
        own = here(src.at[pl.ds(jme * ROW, ROW)], dst.at[pl.ds(jme * ROW, ROW)])
        return cps, own

    def gather_piece(q):
        own_cot[q].wait()
        arrived(cot_cp[q])

        def step(i, carry):
            r = pl.ds(pl.multiple_of(i * 320, 320), 320)
            rows = dot(ohg[r, :], cg[q]) * gc[r, 0:1]
            s[q, r, :] = rows.astype(BF)
            return carry

        lax.fori_loop(0, 2, step, 0)
        sr_cp = spread(s.at[q], sr.at[q])
        return sr_cp, remote(cg.at[q], ch.at[q], dc=1)

    sr_cp, ch_cp = [], []

    def piece(q):
        a, b = gather_piece(q)
        sr_cp.append(a)
        ch_cp.append(b)

    piece(0)
    actx_own.wait()
    arrived(actx_cp)

    def actp_step(i, carry):
        r = pl.ds(pl.multiple_of(i * 320, 320), 320)
        actp[r, :] = dot(pm[r, :], actx[...]).astype(BF)
        return carry

    lax.fori_loop(0, 2, actp_step, 0)
    actr_cp, actr_own = spread(actp, actr)

    for cp in a1_own:
        cp.wait()
    arrived(a1_cp)
    for xt in range(NX):
        a2s[xt] = sum(a1r[k, xt].astype(F32) * hot_z[k] for k in range(4)).astype(BF)
    a2_cp = [remote(a2s.at[(x + d) % 4], a2r.at[x], dx=d) for d in range(1, 4)]
    a2_own = here(a2s.at[x], a2r.at[x])
    piece(1)
    a2_own.wait()
    arrived(a2_cp)
    a3s[...] = sum(a2r[k].astype(F32) * hot_x[k] for k in range(4)).astype(BF)
    a3_cp = remote(a3s, a3r, dyh=1)
    piece(2)
    arrived([a3_cp])
    mine = hot_y[0] * (yh == 0).astype(F32) + hot_y[1] * (yh == 1).astype(F32)
    ags[...] = (a3s[...].astype(F32) * mine + a3r[...].astype(F32) * (1.0 - mine)).astype(BF)
    wh_slot = wh.at[pl.ds(yl * 64 + z * 16, 16)]
    wh_cp = [
        remote(ags, wh_slot, dyl=b, dz=d) for b in range(2) for d in range(4) if b or d
    ]
    wh_own = here(ags, wh_slot)
    piece(3)

    for cp in at_own:
        cp.wait()
    arrived(at_cp)
    wh_own.wait()
    arrived(wh_cp)
    for q in range(NQ):
        arrived([ch_cp[q]])
        for b in range(NX):
            r, t = pl.ds(b * TOK, TOK), pl.ds((4 + b) * TOK, TOK)
            sh[r, :] = (cg[q, r, :].astype(F32) * gh[r, 0:1]).astype(BF)
            sh[t, :] = (ch[q, r, :].astype(F32) * gh[t, 0:1]).astype(BF)
        hp[:, cols(q)] = dot(at[...], sh[...]).astype(BF)
        part = dot(wh[:, cols(q)], sh[...], NT)
        hhacc[...] = part if q == 0 else hhacc[...] + part
    hhs[...] = hhacc[...].astype(BF)
    hh_cp, hh_own = [], []
    for cc in range(2):
        for d in range(4):
            for h in range(2):
                src = hhs.at[pl.ds(64 * h, 64), pl.ds((cc * 4 + (x + d) % 4) * TOK, TOK)]
                dst = hht.at[pl.ds(512 * h + 256 * c + 64 * x, 64)]
                if cc or d:
                    hh_cp.append(remote(src, dst, dx=d, dc=cc))
                else:
                    hh_own.append(here(src, dst))
    rs_cp = []
    k = 1
    for a in range(2):
        for b in range(2):
            for d in range(4):
                src = hp.at[
                    pl.ds(((yl + b) % 2) * 64 + ((z + d) % 4) * 16, 16),
                    pl.ds(((yh + a) % 2) * HALF, HALF),
                ]
                if a or b or d:
                    rs_cp.append(remote(src, rsb.at[k], dyh=a, dyl=b, dz=d))
                    k += 1
                else:
                    rs_own = here(src, rsb.at[0])

    actr_own.wait()
    arrived(actr_cp)
    yr_cp = []
    for q in range(NQ):
        w_copy[q].wait()
        sr_cp[q][1].wait()
        arrived(sr_cp[q][0])

        def wg_step(i, carry):
            r = pl.ds(pl.multiple_of(i * 256, 256), 256)
            wgs[r, :] = dot(actr[:, r], sr[q], TN).astype(BF)
            return carry

        lax.fori_loop(0, 4, wg_step, 0)
        cr_cp = [
            remote(wgs.at[pl.ds(512 * h + 256 * ((c + 1) % 2), 256)], cr.at[q % 2, h], dc=1)
            for h in range(2)
        ]

        def dg_step(i, carry):
            r = pl.ds(pl.multiple_of(i * 256, 256), 256)
            part = dot(sr[q], wq[q, r, :], NT)
            hacc[:, r] = part if q == 0 else hacc[:, r] + part
            return carry

        lax.fori_loop(0, 4, dg_step, 0)
        for cp in cr_cp:
            cp.wait()
        there, stay = (yl + 1) % 2, yl
        if q >= 2:
            yr_cp[q - 2].wait_send()
        ys[q % 2] = (
            wgs[pl.ds(512 * there + 256 * c, 256), :].astype(F32)
            + cr[q % 2, there].astype(F32)
        ).astype(BF)
        yr_cp.append(remote(ys.at[q % 2], yr.at[q], dyl=1))
        wg[:, cols(q)] = (
            wgs[pl.ds(512 * stay + 256 * c, 256), :].astype(F32)
            + cr[q % 2, stay].astype(F32)
        ).astype(BF)
    left(actx_cp)
    hg = acts

    def hg_step(i, carry):
        r = pl.ds(pl.multiple_of(i * 128, 128), 128)
        hg[r, :] = hacc[r, :].astype(BF)
        return carry

    lax.fori_loop(0, 5, hg_step, 0)
    hgx_cp, hgx_own = spread(hg, hgx)

    rs_own.wait()
    arrived(rs_cp)
    gp[...] = sum(rsb[k].astype(F32) for k in range(16)).astype(BF)
    g1_cp = [remote(gp, g1.at[z], dz=d) for d in range(1, 4)]
    g1_own = here(gp, g1.at[z])

    left(actr_cp)
    hgx_own.wait()
    arrived(hgx_cp)
    hgp = actp

    for i in range(5):
        r = pl.ds(i * 128, 128)
        hgp[r, :] = dot(pm[:, r], hgx[...], TN).astype(BF)
    ret_cp = [
        remote(hgp.at[pl.ds(((x + d) % 4) * 160, 160)], ret.at[pl.ds(x * 160, 160)], dx=d)
        for d in (1, 3, 2)
    ]
    ret_own = here(hgp.at[pl.ds(x * 160, 160)], ret.at[pl.ds(x * 160, 160)])

    g1_own.wait()
    arrived(g1_cp)
    g2_cp = remote(g1, g2.at[yh], dyh=1)
    g2_own = here(g1, g2.at[yh])
    for cp in hh_own:
        cp.wait()
    arrived(hh_cp)
    ret[pl.ds(COLD, TOK), :] = dot(eye, hht[...], NT).astype(BF)
    g2_own.wait()
    arrived([g2_cp])
    g3_cp = [remote(g2, g3.at[x], dx=d) for d in (1, 3, 2)]
    g3_own = here(g2, g3.at[x])

    ret_own.wait()
    arrived(ret_cp)

    def out_step(i, carry):
        r = pl.ds(pl.multiple_of(i * 256, 256), 256)
        hid[:, r] = dot(ohx[...], ret[:, r], TN).astype(BF)
        return carry

    lax.fori_loop(0, 4, out_step, 0)

    for q in range(NQ):
        yr_cp[q].wait_recv()
        if q >= 2:
            sent.append(yr_cp[q])
        wg[:, cols(q)] = (wg[:, cols(q)].astype(F32) + yr[q].astype(F32)).astype(BF)
    g3_own.wait()
    arrived(g3_cp)
    own = (e1 == e).astype(F32)
    is_hot = jnp.sum(own * hotv, axis=0, keepdims=True)
    for xt in range(NX):
        for h in range(2):
            for zt in range(NZ):
                r, k = pl.ds(64 * xt + 16 * zt, 16), pl.ds(h * HALF, HALF)
                wg[r, k] = (
                    wg[r, k].astype(F32) * (1.0 - is_hot) + g3[xt, h, zt].astype(F32) * is_hot
                ).astype(BF)
    for cp in sent:
        cp.wait_send()


def vm(*shape, dtype=BF):
    return pltpu.VMEM(shape, dtype)


def run_main(cot, meta, rnat, pre, w):
    anyw = pl.BlockSpec(memory_space=pl.ANY)
    vmem = pl.BlockSpec(memory_space=pltpu.VMEM)
    scratch = [
        vm(NQ, SLOT, DQ), vm(NQ, SLOT, DQ), vm(8, 8, 128, dtype=F32), vm(TOK, TOPK, 2 * HID),
        vm(NQ, HID, DQ),
        vm(COLD + TOK, SLOT), vm(COLD, SLOT), vm(COLD, COLD), vm(COLD, 128, dtype=F32),
        vm(8 * TOK, 128, dtype=F32),
        vm(COLD + TOK, HID), vm(COLD, HID), vm(COLD, HID), vm(COLD, HID),
        vm(NQ, COLD, DQ), vm(NQ, COLD, DQ), vm(COLD, HID, dtype=F32), vm(COLD, HID),
        vm(COLD + TOK, HID),
        vm(HID, DQ), vm(2, 2, 256, DQ), vm(2, 256, DQ), vm(NQ, 256, DQ),
        vm(4, 4, 16, D), vm(4, 16, D), vm(4, 16, D), vm(16, D), vm(16, D), vm(16, D),
        vm(128, D),
        vm(HID, TOK), vm(128, 8 * TOK), vm(HID, TOK), vm(128, 8 * TOK),
        vm(128, 8 * TOK, dtype=F32), vm(8 * TOK, DQ), vm(128, D), vm(16, 16, HALF),
        vm(16, HALF), vm(4, 16, HALF), vm(2, 4, 16, HALF), vm(4, 2, 4, 16, HALF),
        pltpu.SemaphoreType.DMA((192,)), pltpu.SemaphoreType.DMA((192,)),
        pltpu.SemaphoreType.DMA((40,)),
    ]
    return pl.pallas_call(
        main_kernel,
        out_shape=(
            jax.ShapeDtypeStruct((SLOT, HID), BF),
            jax.ShapeDtypeStruct((256, D), BF),
        ),
        in_specs=[anyw, vmem, vmem, anyw, anyw],
        out_specs=(vmem, vmem),
        scratch_shapes=scratch,
        compiler_params=pltpu.CompilerParams(
            collective_id=0, has_side_effects=True, vmem_limit_bytes=60 * 1024 * 1024
        ),
        cost_estimate=pl.CostEstimate(
            flops=22 * 10**9, bytes_accessed=16 * 10**6, transcendentals=10**6
        ),
    )(cot, meta, rnat, pre, w)


def grad_kernel(h, p, o):
    n = h.shape[0]
    back = h[...].astype(F32)
    rows = p[...].reshape(n, 2 * HID).astype(F32)
    gate, up = rows[:, :HID], rows[:, HID:]
    sig = jax.nn.sigmoid(gate)
    left = back * up * sig * (1.0 + gate * (1.0 - sig))
    right = back * gate * sig
    o[:, :, :HID] = left.astype(BF).reshape(n // TOPK, TOPK, HID)
    o[:, :, HID:] = right.astype(BF).reshape(n // TOPK, TOPK, HID)


def run_grad(hidden, pre):
    n = 16
    return pl.pallas_call(
        grad_kernel,
        grid=(TOK // n,),
        out_shape=jax.ShapeDtypeStruct((TOK, TOPK, 2 * HID), BF),
        in_specs=[
            pl.BlockSpec((n * TOPK, HID), lambda i: (i, 0)),
            pl.BlockSpec((n, TOPK, 2 * HID), lambda i: (i, 0, 0)),
        ],
        out_specs=pl.BlockSpec((n, TOPK, 2 * HID), lambda i: (i, 0, 0)),
        compiler_params=pltpu.CompilerParams(vmem_limit_bytes=24 * 1024 * 1024),
    )(hidden, pre)


def local(cotangent, routes, gates, pre_act, down_weight):
    meta = jnp.concatenate([routes.astype(F32).T, gates.T], axis=0)
    rnat = routes.astype(F32).reshape(1, SLOT)
    hidden, weight = run_main(cotangent, meta, rnat, pre_act, down_weight[0])
    return run_grad(hidden, pre_act), weight[None]


def solution(mesh):
    in_specs = (
        P(("grp", "ep"), None),
        P(("grp", "ep"), None),
        P(("grp", "ep"), None),
        P(("grp", "ep"), None, None),
        P("ep", None, None),
    )
    out_specs = (P(("grp", "ep"), None, None), P("ep", "grp", None))
    return jax.shard_map(local, mesh=mesh, in_specs=in_specs, out_specs=out_specs, check_vma=False)
```

time: 656 us -> 228 us (0.35)
  waiting for transfers between devices: 369 us -> 0 us
  Pallas kernels: 0 us -> 221 us
  blocking collectives: 111 us -> 0 us
  local copies, waits for them, and re-layouts: 76.3 us -> 3.25 us
  matrix products: 31.8 us -> 0 us
  other arithmetic: 33.5 us -> 1.96 us
  starting transfers between devices: 18.6 us -> 0 us
  between operations: 14.9 us -> 0.66 us
    psum x1 -> x0, waiting for transfers between devices: 305 us -> none  [from_root(): return lax.psum(kept, axis)]
    pallas_call x0 -> x2, Pallas kernels: none -> 221 us  [the longest x1 217 us: run_main(): pl.pallas_call(main_kernel, out_shape=(jax.ShapeDtypeStruct((SLOT, HID),...]
    all_to_all x1 -> x0, blocking collectives: 111 us -> none  [local(): lax.all_to_all(send_grad, 'ep', split_axis=0, concat_axis=0, tiled=True)]
    gather x8 -> x0, local copies, waits for them, and re-layouts: 38.5 us -> none  [the longest x2 20.5 us: local(): jnp.take(scaled, cold_source, axis=0, mode='fill', fill_value=0)]
    reduce_scatter x1 -> x0, waiting for transfers between devices: 36.3 us -> none  [local(): lax.psum_scatter((jnp.dot(received_act.T, received_grad, preferred_elemen...]
    dot_general x4 -> x0, matrix products: 31.8 us -> none  [the longest x1 11.6 us: local(): jnp.dot(received_act.T, received_grad, preferred_element_type=jnp.float32)]
    all_to_all x2 -> x0, waiting for transfers between devices: 27.1 us -> none  [the longest x1 18.7 us: local(): lax.all_to_all(owner_grad.reshape(ep_size, capacity, hidden), 'ep', split...]
    all_to_all x2 -> x0, starting transfers between devices: 18.5 us -> none  [the longest x1 11.7 us: local(): lax.all_to_all(send_act, 'ep', split_axis=0, concat_axis=0, tiled=True)]
  transfers between devices with their start and end apart: 4 -> 0, of which waited for: 4 -> 0; matrix products, arithmetic and copies ran while one was open for 12% -> 0% of each run, Pallas kernels for 0% -> 0%
where the time goes in v1:
time: 228 us; the launch traced here: 227 us
  Pallas kernels  221 us (97%)
  local copies, waits for them, and re-layouts  3.25 us (1%)
    pallas_call x1, Pallas kernels, run_main(): pl.pallas_call(main_kernel, out_shape=(jax.ShapeDtypeStruct((SLOT, HID),...  217 us

profile of v1, /device:TPU:1, one launch (start us, length us, event | category | flops | bytes accessed | tf_op | source)
XLA Modules:
  0.0 226.9 jit_solution(9852141199636786374)
XLA Ops:
  0.6 0.7 fusion
  1.3 1.3 pad_maximum_fusion.meta
  2.6 0.1 copy.8
  2.7 0.7 reshape.7.rnat
  3.4 0.0 copy-start
  3.4 217.3 %shard_map.68 = (bf16[512,1024]{1,0:T(8,128)(2,1)}, bf16[256,3584]{1,0:T(8,128)(2,1)}) custom-call(bf16[128,3584]{1,0:T(8,128)(2,1)} %cot.1, f32[8,128]{1,0:T(8,128)} %pad_maximum_fusion.meta, f32[1,512]{1,0:T(1,128)} %reshape.7.rnat, bf16[128,4,2048]{2,1,0:T(4,128)(2,1)} %p.1, bf16[1024,3584]{1,0:T(8,128)(2,1)} %bitcast.7), custom_call_target="tpu_custom_call" | custom-call | flops 22000001024 | bytes 16000000 | tf_op jit(solution)/shard_map/pallas_call | solution.py:474
  220.7 0.0 copy-done
  220.7 0.0 copy-start.1
  220.7 1.2 copy-done.1
  221.9 0.0 copy-start.2
  221.9 3.7 %shard_map.69 = bf16[128,4,2048]{2,1,0:T(4,128)(2,1)} custom-call(bf16[512,1024]{1,0:T(8,128)(2,1)S(1)} %copy-done.1, bf16[128,4,2048]{2,1,0:T(4,128)(2,1)S(1)} %copy-done), custom_call_target="tpu_custom_call" | custom-call | tf_op jit(solution)/shard_map/pallas_call | solution.py:506
  225.7 0.0 copy-done.2
  225.7 1.2 copy.10
Async XLA Ops:
  3.4 217.3 %copy-start = (bf16[128,4,2048]{2,1,0:T(4,128)(2,1)S(1)}, bf16[128,4,2048]{2,1,0:T(4,128)(2,1)}, u32[]{:S(2)}) copy-start(bf16[128,4,2048]{2,1,0:T(4,128)(2,1)} %p.1) | copy-start | bytes 6291460
  220.7 1.2 copy-start.1
  221.9 3.7 %copy-start.2 = (bf16[256,3584]{1,0:T(8,128)(2,1)S(1)}, bf16[256,3584]{1,0:T(8,128)(2,1)}, u32[]{:S(2)}) copy-start(bf16[256,3584]{1,0:T(8,128)(2,1)} %get-tuple-element.5) | copy-start | bytes 5505028

commit v2 on v1

v2 whole, which is shorter than its diff:
```python
import functools

import jax
import jax.numpy as jnp
from jax import lax
from jax.experimental import pallas as pl
from jax.experimental.pallas import tpu as pltpu
from jax.sharding import PartitionSpec as P

MESH = pl.DeviceIdType.MESH
BF = jnp.bfloat16
F32 = jnp.float32

TOK = 128
TOPK = 4
SLOT = TOK * TOPK
HID = 1024
D = 3584
CAP = 20
NX, NZ = 4, 4
NJ = 8
NQ = 4
DQ = D // NQ
ROW = NX * CAP
COLD = NJ * ROW
HALF = D // 2
HALFHID = HID // 2


def dot(a, b, dims=((1,), (0,))):
    return lax.dot_general(a, b, (dims, ((), ())), preferred_element_type=F32)


NN = ((1,), (0,))
NT = ((1,), (1,))
TN = ((0,), (0,))


def iota(shape, dim):
    return lax.broadcasted_iota(jnp.int32, shape, dim)


def onehot(flag):
    return flag.astype(F32).astype(BF)


def main_kernel(
    cot, meta, rnat, pre, w,
    hid, wg,
    cg, ch, mg, pa, wq,
    ohx, sel, ohg, pm, px, gc,
    acts, actx, actp, actr, actb,
    s, sr, sp, hacc, hgx, ret,
    wgs, cr, ys, yr,
    a1r, a2s, a2r, a3s, a3r, ags, wh,
    ahot, aht, at, hht, hhs, hp, rsb, gp, g1, g2, g3,
    ssem, rsem, lsem,
):
    g, e = lax.axis_index("grp"), lax.axis_index("ep")
    yl, c = g // 2, g % 2
    x, yh, z = e // 8, (e // 4) % 2, e % 4
    us, vs = (x, z), (z, x)

    def dev(dx=0, dyh=0, dz=0, dyl=0, dc=0):
        return (
            ((yl + dyl) % 2) * 2 + (c + dc) % 2,
            (((x + dx) % 4) * 2 + (yh + dyh) % 2) * 4 + (z + dz) % 4,
        )

    def way(p, du=0, dv=0, **to):
        return dict(dx=(du, dv)[p], dz=(dv, du)[p], **to)

    counts = [0, 0]

    def remote(src, dst, **to):
        k = counts[0]
        counts[0] += 1
        cp = pltpu.make_async_remote_copy(
            src_ref=src, dst_ref=dst, send_sem=ssem.at[k], recv_sem=rsem.at[k],
            device_id=dev(**to), device_id_type=MESH,
        )
        cp.start()
        return cp

    def here(src, dst):
        k = counts[1]
        counts[1] += 1
        cp = pltpu.make_async_copy(src, dst, lsem.at[k])
        cp.start()
        return cp

    sent = []

    def arrived(copies):
        for cp in copies:
            cp.wait_recv()
        sent.extend(copies)

    def left(copies):
        gone = [id(cp) for cp in copies]
        sent[:] = [cp for cp in sent if id(cp) not in gone]
        for cp in copies:
            cp.wait_send()

    def cols(q):
        return pl.ds(q * DQ, DQ)

    def half(p):
        return pl.ds(p * HALF, HALF)

    def hh(p):
        return pl.ds(p * HALFHID, HALFHID)

    peers = set()
    for p in range(2):
        for d in range(4):
            for a in range(2):
                for b in range(2):
                    peers.add(tuple(sorted(way(p, dv=d, dyh=a, dyl=b, dc=0).items())))
            for cc in range(2):
                peers.add(tuple(sorted(way(p, du=d, dyh=0, dyl=0, dc=cc).items())))
    peers = [dict(t) for t in sorted(peers) if any(v for _, v in t)]
    barrier = pltpu.get_barrier_semaphore()
    for to in peers:
        pl.semaphore_signal(barrier, inc=1, device_id=dev(**to), device_id_type=MESH)
    ORDER = (0, 2, 1, 3)
    own_cot = {}
    for q in ORDER:
        own_cot[q] = here(cot.at[:, cols(q)], cg.at[q, pl.ds(us[q // 2] * TOK, TOK)])
    NP = 4
    pt = TOK // NP
    pa_copy = [here(pre.at[pl.ds(i * pt, pt)], pa.at[i]) for i in range(2)]
    pl.semaphore_wait(barrier, len(peers))

    cot_cp = {}

    def send_cot(q):
        p = q // 2
        cot_cp[q] = [
            remote(cot.at[:, cols(q)], cg.at[q, pl.ds(us[p] * TOK, TOK)], **way(p, du=d))
            for d in (1, 3, 2)
        ]

    meta_cp = []
    for p in range(2):
        for cc in range(2):
            for d in range(4):
                if cc or d:
                    meta_cp.append(remote(meta, mg.at[p, cc * 4 + us[p]], **way(p, du=d, dc=cc)))
    send_cot(0)
    send_cot(2)
    for p in range(2):
        mg[p, us[p]] = meta[...]

    rn = rnat[...]
    ei = iota((32, SLOT), 0)
    eid = ei.astype(F32)
    member = (rn == eid).astype(F32)
    tri = onehot(iota((SLOT, SLOT), 0) < iota((SLOT, SLOT), 1))
    rank = dot(member.astype(BF), tri)
    hotv = (jnp.sum(member, axis=1, keepdims=True) >= 64.0).astype(F32)
    token = lax.shift_right_logical(iota((32, SLOT), 1), 2).astype(F32)
    turned = ((ei & 3) * 8 + (ei & 4) + lax.shift_right_logical(ei, 3)).astype(F32)
    cold = member * (1.0 - hotv)
    for p in range(2):
        order = (eid, turned)[p]
        key = jnp.sum(cold * (order * CAP + rank) - (member - cold), axis=0, keepdims=True)
        for i in range(COLD // 128):
            ohx[p, pl.ds(i * 128, 128), :] = onehot(
                iota((128, SLOT), 0).astype(F32) + i * 128.0 == key
            )
    key = jnp.sum(member * hotv * (token + 1.0), axis=0, keepdims=True) - 1.0
    sel[...] = onehot(iota((128, SLOT), 0).astype(F32) == key)
    e1 = iota((32, 1), 0)

    def hot_is(flag):
        return jnp.sum(hotv * flag.astype(F32), axis=0, keepdims=True)

    hotid = jnp.sum(hotv * e1.astype(F32), axis=0, keepdims=True)
    hot_x = [hot_is(lax.shift_right_logical(e1, 3) == k) for k in range(4)]
    hot_z = [hot_is((e1 & 3) == k) for k in range(4)]
    hot_y = [hot_is((lax.shift_right_logical(e1, 2) & 1) == k) for k in range(2)]
    hot_u, hot_v = (hot_x, hot_z), (hot_z, hot_x)

    send_cot(1)
    send_cot(3)
    a1_cp, a1_own = [], []
    for p in range(2):
        a1_cp.append([
            remote(w.at[yl, c, :, (vs[p] + d) % 4, :, half(p)], a1r.at[p, vs[p]], **way(p, dv=d))
            for d in (1, 3, 2)
        ])
        a1_own.append(here(w.at[yl, c, :, vs[p], :, half(p)], a1r.at[p, vs[p]]))
    w_copy = {q: here(w.at[:, :, :, :, :, cols(q)], wq.at[q]) for q in ORDER}

    for i in range(NP):
        pa_copy[i].wait()

        def act_step(j, carry):
            rows = pa[i % 2, pl.ds(j * 8, 8)].reshape(32, 2 * HID).astype(F32)
            gate, up = rows[:, :HID], rows[:, HID:]
            hid[pl.ds(pl.multiple_of(i * pt * 4 + j * 32, 32), 32), :] = (
                gate * jax.nn.sigmoid(gate) * up
            ).astype(BF)
            return carry

        lax.fori_loop(0, pt // 8, act_step, 0)
        if i + 2 < NP:
            pa_copy.append(here(pre.at[pl.ds((i + 2) * pt, pt)], pa.at[i % 2]))

    actx_cp, actx_own = [], []
    for p in range(2):

        def acts_step(i, carry):
            r = pl.ds(pl.multiple_of(i * 320, 320), 320)
            acts[p, r, :] = dot(ohx[p, r, :], hid[:, hh(p)]).astype(BF)
            return carry

        lax.fori_loop(0, 2, acts_step, 0)
        u = us[p]
        actx_cp.append([
            remote(acts.at[p, pl.ds(((u + d) % 4) * 160, 160)], actx.at[p, pl.ds(u * 160, 160)],
                   **way(p, du=d))
            for d in (1, 3, 2)
        ])
        actx_own.append(here(acts.at[p, pl.ds(u * 160, 160)], actx.at[p, pl.ds(u * 160, 160)]))
    ahot[...] = dot(sel[...], hid[...]).astype(BF)
    eye = onehot(iota((TOK, TOK), 0) == iota((TOK, TOK), 1))
    aht[...] = dot(ahot[...], eye, TN).astype(BF).reshape(2, HID // 2, TOK)

    def ring_part(p, d, cc):
        return pl.ds(256 * ((c + cc) % 2) + 64 * ((us[p] + d) % 4), 64)

    at_cp, at_own = [], []
    for p in range(2):
        at_cp.append([])
        for cc in range(2):
            for d in range(4):
                src = aht.at[:, ring_part(p, d, cc), :]
                dst = at.at[p, :, :, pl.ds((cc * 4 + us[p]) * TOK, TOK)]
                if cc or d:
                    at_cp[p].append(remote(src, dst, **way(p, du=d, dc=cc)))
                else:
                    at_own.append(here(src, dst))

    arrived(meta_cp)
    tri1 = onehot(iota((TOK, TOK), 0) < iota((TOK, TOK), 1))
    i8 = iota((NJ, TOK), 0)
    rows80 = iota((ROW, SLOT), 0).astype(F32)
    for p in range(2):
        if p == 0:
            ej = (i8 + 8 * x).astype(F32)
        else:
            ej = ((i8 & 3) * 8 + (i8 & 4) + z).astype(F32)
        keys, gates8 = [], []
        for b in range(NX):
            m = mg[p, b]
            hit = [(m[k:k + 1] == ej) for k in range(TOPK)]
            mem8 = sum(f.astype(F32) for f in hit)
            gates8.append(sum(jnp.where(hit[k], m[4 + k:5 + k], 0.0) for k in range(TOPK)))
            rank8 = dot(mem8.astype(BF), tri1)
            mem8 = mem8 * (ej != hotid).astype(F32)
            keys.append(jnp.where(mem8 > 0, rank8 + CAP * b, -1.0))
        keys = jnp.concatenate(keys, axis=1)
        gates8 = jnp.concatenate(gates8, axis=1)
        for j in range(NJ):
            flag = rows80 == keys[j:j + 1]
            ohg[p, pl.ds(j * ROW, ROW), :] = onehot(flag)
            col = jnp.sum(jnp.where(flag, gates8[j:j + 1], 0.0), axis=1, keepdims=True)
            gc[p, pl.ds(j * ROW, ROW), :] = jnp.broadcast_to(col, (ROW, 128))

    def spread(p, src, dst):
        v = vs[p]
        cps = [
            remote(
                src.at[pl.ds((((yh + a) % 2) * 4 + (v + d) % 4) * ROW, ROW)],
                dst.at[pl.ds((yh * 4 + v) * ROW, ROW)], **way(p, dv=d, dyh=a, dyl=a),
            )
            for a, d in ((0, 1), (0, 3), (1, 0), (0, 2), (1, 1), (1, 3), (1, 2))
        ]
        own = pl.ds((yh * 4 + v) * ROW, ROW)
        return cps, here(src.at[own], dst.at[own])

    sr_cp, ch_cp = {}, {}

    def piece(q):
        p = q // 2
        own_cot[q].wait()
        arrived(cot_cp[q])

        def step(i, carry):
            r = pl.ds(pl.multiple_of(i * 320, 320), 320)
            s[q, r, :] = (dot(ohg[p, r, :], cg[q]) * gc[p, r, 0:1]).astype(BF)
            return carry

        lax.fori_loop(0, 2, step, 0)
        sr_cp[q] = spread(p, s.at[q], sr.at[q])
        ch_cp[q] = remote(cg.at[q], ch.at[q], dc=1)

    piece(0)
    piece(2)
    o = iota((COLD, 128), 0)
    oj = sum((o >= ROW * k).astype(jnp.int32) for k in range(1, NJ))
    orem = o - ROW * oj
    ob = sum((orem >= CAP * k).astype(jnp.int32) for k in range(1, NX))
    want = ob * 160 + oj * CAP + (orem - CAP * ob)
    for k in range(COLD // 128):
        pm[:, pl.ds(k * 128, 128)] = onehot(want == iota((COLD, 128), 1) + k * 128)
    o = iota((4 * ROW, 4 * ROW), 0)
    oj = sum((o >= ROW * k).astype(jnp.int32) for k in range(1, 4))
    orem = o - ROW * oj
    ob = sum((orem >= CAP * k).astype(jnp.int32) for k in range(1, NX))
    px[...] = onehot(ob * ROW + oj * CAP + (orem - CAP * ob) == iota((4 * ROW, 4 * ROW), 1))

    def turn(src, dst):
        for k in range(2):
            r = pl.ds(k * 4 * ROW, 4 * ROW)
            dst[r, :] = dot(px[...], src[r, :]).astype(BF)

    actr_cp, actr_own = [], []
    for p in range(2):
        actx_own[p].wait()
        arrived(actx_cp[p])

        def actp_step(i, carry):
            r = pl.ds(pl.multiple_of(i * 320, 320), 320)
            actp[p, r, :] = dot(pm[r, :], actx[p]).astype(BF)
            return carry

        lax.fori_loop(0, 2, actp_step, 0)
        a, b = spread(p, actp.at[p], actr.at[p])
        actr_cp.append(a)
        actr_own.append(b)

    a2_cp, a2_own, a3_cp, wh_cp, wh_own = [], [], [], [], []
    for p in range(2):
        a1_own[p].wait()
        arrived(a1_cp[p])
        for k in range(4):
            a2s[p, k] = sum(a1r[p, i, k].astype(F32) * hot_v[p][i] for i in range(4)).astype(BF)
        u = us[p]
        a2_cp.append([
            remote(a2s.at[p, (u + d) % 4], a2r.at[p, u], **way(p, du=d)) for d in (1, 3, 2)
        ])
        a2_own.append(here(a2s.at[p, u], a2r.at[p, u]))
    piece(1)
    for p in range(2):
        a2_own[p].wait()
        arrived(a2_cp[p])
        a3s[p] = sum(a2r[p, k].astype(F32) * hot_u[p][k] for k in range(4)).astype(BF)
        a3_cp.append(remote(a3s.at[p], a3r.at[p], dyh=1))
    piece(3)
    mine = hot_y[0] * (yh == 0).astype(F32) + hot_y[1] * (yh == 1).astype(F32)
    for p in range(2):
        arrived([a3_cp[p]])
        ags[p] = (
            a3s[p].astype(F32) * mine + a3r[p].astype(F32) * (1.0 - mine)
        ).astype(BF)
        slot = wh.at[p, yl, vs[p]]
        wh_cp.append([
            remote(ags.at[p], slot, **way(p, dv=d, dyl=b))
            for b in range(2) for d in range(4) if b or d
        ])
        wh_own.append(here(ags.at[p], slot))

    sh = wgs
    diag = iota((TOK, TOK), 0) == iota((TOK, TOK), 1)
    hh_cp, hh_own, rs_cp, rs_own = [], [], [], []
    for p in range(2):
        at_own[p].wait()
        arrived(at_cp[p])
        wh_own[p].wait()
        arrived(wh_cp[p])
        for i in range(2):
            q = 2 * p + i
            arrived([ch_cp[q]])
            for b in range(2 * NX):
                m = mg[p, b]
                row = sum(
                    jnp.where(m[k:k + 1] == hotid, m[4 + k:5 + k], 0.0) for k in range(TOPK)
                )
                col = jnp.sum(jnp.where(diag, row, 0.0), axis=1, keepdims=True)
                block = (cg, ch)[b // NX][q, pl.ds((b % NX) * TOK, TOK), :]
                sh[pl.ds(b * TOK, TOK), :] = (block.astype(F32) * col).astype(BF)
            hp[q] = dot(at[p].reshape(128, 8 * TOK), sh[...]).astype(BF)
            part = dot(wh[p, :, :, :, pl.ds(i * DQ, DQ)].reshape(128, DQ), sh[...], NT)
            hacc[0:128, :] = part if i == 0 else hacc[0:128, :] + part
        hhs[p] = hacc[0:128, :].astype(BF).reshape(2, 64, 8 * TOK)
        hh_cp.append([])
        for cc in range(2):
            for d in range(4):
                src = hhs.at[p, :, :, pl.ds((cc * 4 + (us[p] + d) % 4) * TOK, TOK)]
                dst = hht.at[p, :, pl.ds(256 * c + 64 * us[p], 64), :]
                if cc or d:
                    hh_cp[p].append(remote(src, dst, **way(p, du=d, dc=cc)))
                else:
                    hh_own.append(here(src, dst))
        rs_cp.append([])
        k = 1
        for a in range(2):
            for b in range(2):
                for d in range(4):
                    src = hp.at[
                        2 * p + (yh + a) % 2,
                        pl.ds(((yl + b) % 2) * 64 + ((vs[p] + d) % 4) * 16, 16),
                    ]
                    if a or b or d:
                        rs_cp[p].append(
                            remote(src, rsb.at[p, k], **way(p, dv=d, dyh=a, dyl=b))
                        )
                        k += 1
                    else:
                        rs_own.append(here(src, rsb.at[p, 0]))

    for p in range(2):
        actr_own[p].wait()
        arrived(actr_cp[p])
    turn(actr.at[1], actb)
    yr_cp = {}
    last_ys = {}
    for n, q in enumerate(ORDER):
        w_copy[q].wait()
        sr_cp[q][1].wait()
        arrived(sr_cp[q][0])
        rows = sr.at[q]
        if q >= 2:
            turn(sr.at[q], sp)
            rows = sp

        for p in range(2):
            act = (actr.at[0], actb)[p]

            def wg_step(i, carry):
                r = pl.ds(pl.multiple_of(i * 256, 256), 256)
                wgs[pl.ds(pl.multiple_of(p * HALFHID + i * 256, 256), 256), :] = dot(
                    act[:, r], rows[...], TN
                ).astype(BF)
                return carry

            lax.fori_loop(0, 2, wg_step, 0)
        cr_cp = [
            remote(wgs.at[pl.ds(512 * h + 256 * ((c + 1) % 2), 256)], cr.at[n % 2, h], dc=1)
            for h in range(2)
        ]

        for h in range(2):
            for k in range(2):
                r = pl.ds(512 * h + 256 * k, 256)
                part = dot(rows[...], wq[q, h, k].reshape(256, DQ), NT)
                hacc[:, r] = part if n == 0 else hacc[:, r] + part
        for cp in cr_cp:
            cp.wait()
        there, stay = (yl + 1) % 2, yl
        if n >= 2:
            yr_cp[ORDER[n - 2]].wait_send()
        ys[n % 2] = (
            wgs[pl.ds(512 * there + 256 * c, 256), :].astype(F32)
            + cr[n % 2, there].astype(F32)
        ).astype(BF)
        yr_cp[q] = remote(ys.at[n % 2], yr.at[q], dyl=1)
        wg[:, cols(q)] = (
            wgs[pl.ds(512 * stay + 256 * c, 256), :].astype(F32)
            + cr[n % 2, stay].astype(F32)
        ).astype(BF)
    for p in range(2):
        left(actx_cp[p])
    hg = acts
    hgx_cp, hgx_own = [], []
    for p in range(2):
        if p == 0:
            hg[0] = hacc[:, hh(0)].astype(BF)
        else:
            for k in range(2):
                r = pl.ds(k * 4 * ROW, 4 * ROW)
                hg[1, r, :] = dot(px[...], hacc[r, hh(1)].astype(BF)).astype(BF)
        a, b = spread(p, hg.at[p], hgx.at[p])
        hgx_cp.append(a)
        hgx_own.append(b)

    g1_cp, g1_own, g2_cp, g2_own, g3_cp, g3_own = [], [], [], [], [], []
    for p in range(2):
        rs_own[p].wait()
        arrived(rs_cp[p])
        gp[p] = sum(rsb[p, k].astype(F32) for k in range(16)).astype(BF)
        g1_cp.append([remote(gp.at[p], g1.at[p, vs[p]], **way(p, dv=d)) for d in (1, 3, 2)])
        g1_own.append(here(gp.at[p], g1.at[p, vs[p]]))

    hgp = actp
    ret_cp, ret_own = [], []
    for p in range(2):
        left(actr_cp[p])
        hgx_own[p].wait()
        arrived(hgx_cp[p])
        for i in range(5):
            r = pl.ds(i * 128, 128)
            hgp[p, r, :] = dot(pm[:, r], hgx[p], TN).astype(BF)
        u = us[p]
        ret_cp.append([
            remote(hgp.at[p, pl.ds(((u + d) % 4) * 160, 160)], ret.at[p, pl.ds(u * 160, 160)],
                   **way(p, du=d))
            for d in (1, 3, 2)
        ])
        ret_own.append(here(hgp.at[p, pl.ds(u * 160, 160)], ret.at[p, pl.ds(u * 160, 160)]))

    for p in range(2):
        g1_own[p].wait()
        arrived(g1_cp[p])
        g2_cp.append(remote(g1.at[p], g2.at[p, yh], dyh=1))
        g2_own.append(here(g1.at[p], g2.at[p, yh]))
    for p in range(2):
        hh_own[p].wait()
        arrived(hh_cp[p])
    ahot[...] = (
        dot(eye, hht[0].reshape(HID, TOK), NT) + dot(eye, hht[1].reshape(HID, TOK), NT)
    ).astype(BF)
    for p in range(2):
        g2_own[p].wait()
        arrived([g2_cp[p]])
        g3_cp.append([remote(g2.at[p], g3.at[p, us[p]], **way(p, du=d)) for d in (1, 3, 2)])
        g3_own.append(here(g2.at[p], g3.at[p, us[p]]))

    for p in range(2):
        ret_own[p].wait()
        arrived(ret_cp[p])
        for i in range(2):
            r, t = pl.ds(i * 256, 256), pl.ds(p * HALFHID + i * 256, 256)
            hid[:, t] = (dot(ohx[p], ret[p, :, r], TN) + dot(sel[...], ahot[:, t], TN)).astype(BF)

    for n, q in enumerate(ORDER):
        yr_cp[q].wait_recv()
        if n >= 2:
            sent.append(yr_cp[q])
        wg[:, cols(q)] = (wg[:, cols(q)].astype(F32) + yr[q].astype(F32)).astype(BF)
    own = (e1 == e).astype(F32)
    is_hot = jnp.sum(own * hotv, axis=0, keepdims=True)
    for p in range(2):
        g3_own[p].wait()
        arrived(g3_cp[p])
        for ut in range(4):
            for i in range(2):
                for vt in range(4):
                    r, k = pl.ds(64 * ut + 16 * vt, 16), cols(2 * p + i)
                    wg[r, k] = (
                        wg[r, k].astype(F32) * (1.0 - is_hot)
                        + g3[p, ut, i, vt].astype(F32) * is_hot
                    ).astype(BF)
    for cp in sent:
        cp.wait_send()


def vm(*shape, dtype=BF):
    return pltpu.VMEM(shape, dtype)


def run_main(cot, meta, rnat, pre, w):
    anyw = pl.BlockSpec(memory_space=pl.ANY)
    vmem = pl.BlockSpec(memory_space=pltpu.VMEM)
    scratch = [
        vm(NQ, SLOT, DQ), vm(NQ, SLOT, DQ), vm(2, 8, 8, 128, dtype=F32),
        vm(2, TOK // 4, TOPK, 2 * HID), vm(NQ, 2, 2, 4, 4, 16, DQ),
        vm(2, COLD, SLOT), vm(TOK, SLOT), vm(2, COLD, SLOT), vm(COLD, COLD),
        vm(4 * ROW, 4 * ROW), vm(2, COLD, 128, dtype=F32),
        vm(2, COLD, HALFHID), vm(2, COLD, HALFHID), vm(2, COLD, HALFHID), vm(2, COLD, HALFHID),
        vm(COLD, HALFHID),
        vm(NQ, COLD, DQ), vm(NQ, COLD, DQ), vm(COLD, DQ), vm(COLD, HID, dtype=F32),
        vm(2, COLD, HALFHID), vm(2, COLD, HALFHID),
        vm(HID, DQ), vm(2, 2, 256, DQ), vm(2, 256, DQ), vm(NQ, 256, DQ),
        vm(2, 4, 4, 16, HALF), vm(2, 4, 16, HALF), vm(2, 4, 16, HALF),
        vm(2, 16, HALF), vm(2, 16, HALF), vm(2, 16, HALF), vm(2, 2, 4, 16, HALF),
        vm(TOK, HID), vm(2, HID // 2, TOK), vm(2, 2, 64, 8 * TOK), vm(2, 2, HID // 2, TOK),
        vm(2, 2, 64, 8 * TOK), vm(NQ, 128, DQ),
        vm(2, 16, 16, DQ), vm(2, 16, DQ), vm(2, 4, 16, DQ), vm(2, 2, 4, 16, DQ),
        vm(2, 4, 2, 4, 16, DQ),
        pltpu.SemaphoreType.DMA((256,)), pltpu.SemaphoreType.DMA((256,)),
        pltpu.SemaphoreType.DMA((64,)),
    ]
    return pl.pallas_call(
        main_kernel,
        out_shape=(
            jax.ShapeDtypeStruct((SLOT, HID), BF),
            jax.ShapeDtypeStruct((256, D), BF),
        ),
        in_specs=[anyw, vmem, vmem, anyw, anyw],
        out_specs=(vmem, vmem),
        scratch_shapes=scratch,
        compiler_params=pltpu.CompilerParams(
            collective_id=0, has_side_effects=True, vmem_limit_bytes=61 * 1024 * 1024
        ),
        cost_estimate=pl.CostEstimate(
            flops=22 * 10**9, bytes_accessed=16 * 10**6, transcendentals=10**6
        ),
    )(cot, meta, rnat, pre, w)


def grad_kernel(h, p, o):
    n = h.shape[0]
    back = h[...].astype(F32)
    rows = p[...].reshape(n, 2 * HID).astype(F32)
    gate, up = rows[:, :HID], rows[:, HID:]
    sig = jax.nn.sigmoid(gate)
    left = back * up * sig * (1.0 + gate * (1.0 - sig))
    right = back * gate * sig
    o[:, :, :HID] = left.astype(BF).reshape(n // TOPK, TOPK, HID)
    o[:, :, HID:] = right.astype(BF).reshape(n // TOPK, TOPK, HID)


def run_grad(hidden, pre):
    n = 16
    return pl.pallas_call(
        grad_kernel,
        grid=(TOK // n,),
        out_shape=jax.ShapeDtypeStruct((TOK, TOPK, 2 * HID), BF),
        in_specs=[
            pl.BlockSpec((n * TOPK, HID), lambda i: (i, 0)),
            pl.BlockSpec((n, TOPK, 2 * HID), lambda i: (i, 0, 0)),
        ],
        out_specs=pl.BlockSpec((n, TOPK, 2 * HID), lambda i: (i, 0, 0)),
        compiler_params=pltpu.CompilerParams(vmem_limit_bytes=24 * 1024 * 1024),
    )(hidden, pre)


def local(cotangent, routes, gates, pre_act, down_weight):
    meta = jnp.concatenate([routes.astype(F32).T, gates.T], axis=0)
    rnat = routes.astype(F32).reshape(1, SLOT)
    hidden, weight = run_main(
        cotangent, meta, rnat, pre_act, down_weight.reshape(2, 2, 4, 4, 16, D)
    )
    return run_grad(hidden, pre_act), weight[None]


def solution(mesh):
    in_specs = (
        P(("grp", "ep"), None),
        P(("grp", "ep"), None),
        P(("grp", "ep"), None),
        P(("grp", "ep"), None, None),
        P("ep", None, None),
    )
    out_specs = (P(("grp", "ep"), None, None), P("ep", "grp", None))
    return jax.shard_map(local, mesh=mesh, in_specs=in_specs, out_specs=out_specs, check_vma=False)
```

time: 228 us -> 179 us (0.79)
  Pallas kernels: 221 us -> 173 us
    pallas_call x1, Pallas kernels: 217 us -> 170 us  [run_main(): pl.pallas_call(main_kernel, out_shape=(jax.ShapeDtypeStruct((SLOT, HID),...]
where the time goes in v2:
time: 179 us
  Pallas kernels  173 us (97%)
  local copies, waits for them, and re-layouts  3.25 us (2%)
  other arithmetic  1.96 us (1%)
    pallas_call x1, Pallas kernels, run_main(): pl.pallas_call(main_kernel, out_shape=(jax.ShapeDtypeStruct((SLOT, HID),...  170 us
    pallas_call x1, Pallas kernels, run_grad(): pl.pallas_call(grad_kernel, grid=(TOK // n,), out_shape=jax.ShapeDtypeStr...  3.74 us

profile of v2, /device:TPU:1, one launch (start us, length us, event | category | flops | bytes accessed | tf_op | source)
XLA Modules:
  0.0 179.1 jit_solution(5016003842100861262)
XLA Ops:
  0.6 0.7 fusion
  1.3 1.3 pad_maximum_fusion.meta
  2.6 0.1 copy.8
  2.7 0.7 reshape.10.rnat
  3.4 0.0 copy-start
  3.4 169.5 %shard_map.68 = (bf16[512,1024]{1,0:T(8,128)(2,1)}, bf16[256,3584]{1,0:T(8,128)(2,1)}) custom-call(bf16[128,3584]{1,0:T(8,128)(2,1)} %cot.1, f32[8,128]{1,0:T(8,128)} %pad_maximum_fusion.meta, f32[1,512]{1,0:T(1,128)} %reshape.10.rnat, bf16[128,4,2048]{2,1,0:T(4,128)(2,1)} %p.1, bf16[2,2,4,4,16,3584]{5,4,3,2,1,0:T(8,128)(2,1)} %bitcast.7), custom_call_target="tpu_custom_call" | custom-call | flops 22000001024 | bytes 16000000 | tf_op jit(solution)/shard_map/pallas_call | solution.py:577
  172.9 0.0 copy-done
  172.9 0.0 copy-start.1
  172.9 1.2 copy-done.1
  174.1 0.0 copy-start.2
  174.2 3.7 %shard_map.69 = bf16[128,4,2048]{2,1,0:T(4,128)(2,1)} custom-call(bf16[512,1024]{1,0:T(8,128)(2,1)S(1)} %copy-done.1, bf16[128,4,2048]{2,1,0:T(4,128)(2,1)S(1)} %copy-done), custom_call_target="tpu_custom_call" | custom-call | tf_op jit(solution)/shard_map/pallas_call | solution.py:609
  177.9 0.0 copy-done.2
  177.9 1.2 copy.10
Async XLA Ops:
  3.4 169.5 %copy-start = (bf16[128,4,2048]{2,1,0:T(4,128)(2,1)S(1)}, bf16[128,4,2048]{2,1,0:T(4,128)(2,1)}, u32[]{:S(2)}) copy-start(bf16[128,4,2048]{2,1,0:T(4,128)(2,1)} %p.1) | copy-start | bytes 6291460
  172.9 1.2 copy-start.1
  174.1 3.7 %copy-start.2 = (bf16[256,3584]{1,0:T(8,128)(2,1)S(1)}, bf16[256,3584]{1,0:T(8,128)(2,1)}, u32[]{:S(2)}) copy-start(bf16[256,3584]{1,0:T(8,128)(2,1)} %get-tuple-element.5) | copy-start | bytes 5505028

commit v3 on v2

--- a/solution.py
+++ b/solution.py
@@ -45,13 +45,13 @@
 
 
 def main_kernel(
-    cot, meta, rnat, pre, w,
+    cot, rt, gt, pre, w,
     hid, wg,
-    cg, ch, mg, pa, wq,
+    meta, cg, ch, mg, pa, wq,
     ohx, sel, ohg, pm, px, gc,
     acts, actx, actp, actr, actb,
     s, sr, sp, hacc, hgx, ret,
-    wgs, cr, ys, yr,
+    wgs, cr, yr,
     a1r, a2s, a2r, a3s, a3r, ags, wh,
     ahot, aht, at, hht, hhs, hp, rsb, gp, g1, g2, g3,
     ssem, rsem, lsem,
@@ -130,6 +130,8 @@
     NP = 4
     pt = TOK // NP
     pa_copy = [here(pre.at[pl.ds(i * pt, pt)], pa.at[i]) for i in range(2)]
+    meta[0:TOPK, :] = rt[...].astype(F32)
+    meta[TOPK:2 * TOPK, :] = gt[...]
     pl.semaphore_wait(barrier, len(peers))
 
     cot_cp = {}
@@ -138,8 +140,18 @@
         p = q // 2
         cot_cp[q] = [
             remote(cot.at[:, cols(q)], cg.at[q, pl.ds(us[p] * TOK, TOK)], **way(p, du=d))
-            for d in (1, 3, 2)
+            for d in (1, 3)
         ]
+
+    fwd_cp = {}
+
+    def pass_on(q):
+        p = q // 2
+        arrived(cot_cp[q])
+        fwd_cp[q] = []
+        for d, k in ((1, 0), (3, TOK // 2)):
+            r = pl.ds(((us[p] - d + 4) % 4) * TOK + k, TOK // 2)
+            fwd_cp[q].append(remote(cg.at[q, r], cg.at[q, r], **way(p, du=d)))
 
     meta_cp = []
     for p in range(2):
@@ -152,7 +164,13 @@
     for p in range(2):
         mg[p, us[p]] = meta[...]
 
-    rn = rnat[...]
+    rn = jnp.zeros((8, SLOT), F32)
+    for k in range(TOPK):
+        rn = rn + dot(
+            jnp.broadcast_to(meta[k:k + 1], (8, TOK)).astype(BF),
+            onehot(iota((TOK, SLOT), 1) == iota((TOK, SLOT), 0) * TOPK + k),
+        )
+    rn = rn[0:1]
     ei = iota((32, SLOT), 0)
     eid = ei.astype(F32)
     member = (rn == eid).astype(F32)
@@ -182,66 +200,11 @@
     hot_y = [hot_is((lax.shift_right_logical(e1, 2) & 1) == k) for k in range(2)]
     hot_u, hot_v = (hot_x, hot_z), (hot_z, hot_x)
 
+    pass_on(0)
+    pass_on(2)
     send_cot(1)
     send_cot(3)
-    a1_cp, a1_own = [], []
-    for p in range(2):
-        a1_cp.append([
-            remote(w.at[yl, c, :, (vs[p] + d) % 4, :, half(p)], a1r.at[p, vs[p]], **way(p, dv=d))
-            for d in (1, 3, 2)
-        ])
-        a1_own.append(here(w.at[yl, c, :, vs[p], :, half(p)], a1r.at[p, vs[p]]))
     w_copy = {q: here(w.at[:, :, :, :, :, cols(q)], wq.at[q]) for q in ORDER}
-
-    for i in range(NP):
-        pa_copy[i].wait()
-
-        def act_step(j, carry):
-            rows = pa[i % 2, pl.ds(j * 8, 8)].reshape(32, 2 * HID).astype(F32)
-            gate, up = rows[:, :HID], rows[:, HID:]
-            hid[pl.ds(pl.multiple_of(i * pt * 4 + j * 32, 32), 32), :] = (
-                gate * jax.nn.sigmoid(gate) * up
-            ).astype(BF)
-            return carry
-
-        lax.fori_loop(0, pt // 8, act_step, 0)
-        if i + 2 < NP:
-            pa_copy.append(here(pre.at[pl.ds((i + 2) * pt, pt)], pa.at[i % 2]))
-
-    actx_cp, actx_own = [], []
-    for p in range(2):
-
-        def acts_step(i, carry):
-            r = pl.ds(pl.multiple_of(i * 320, 320), 320)
-            acts[p, r, :] = dot(ohx[p, r, :], hid[:, hh(p)]).astype(BF)
-            return carry
-
-        lax.fori_loop(0, 2, acts_step, 0)
-        u = us[p]
-        actx_cp.append([
-            remote(acts.at[p, pl.ds(((u + d) % 4) * 160, 160)], actx.at[p, pl.ds(u * 160, 160)],
-                   **way(p, du=d))
-            for d in (1, 3, 2)
-        ])
-        actx_own.append(here(acts.at[p, pl.ds(u * 160, 160)], actx.at[p, pl.ds(u * 160, 160)]))
-    ahot[...] = dot(sel[...], hid[...]).astype(BF)
-    eye = onehot(iota((TOK, TOK), 0) == iota((TOK, TOK), 1))
-    aht[...] = dot(ahot[...], eye, TN).astype(BF).reshape(2, HID // 2, TOK)
-
-    def ring_part(p, d, cc):
-        return pl.ds(256 * ((c + cc) % 2) + 64 * ((us[p] + d) % 4), 64)
-
-    at_cp, at_own = [], []
-    for p in range(2):
-        at_cp.append([])
-        for cc in range(2):
-            for d in range(4):
-                src = aht.at[:, ring_part(p, d, cc), :]
-                dst = at.at[p, :, :, pl.ds((cc * 4 + us[p]) * TOK, TOK)]
-                if cc or d:
-                    at_cp[p].append(remote(src, dst, **way(p, du=d, dc=cc)))
-                else:
-                    at_own.append(here(src, dst))
 
     arrived(meta_cp)
     tri1 = onehot(iota((TOK, TOK), 0) < iota((TOK, TOK), 1))
@@ -286,7 +249,7 @@
     def piece(q):
         p = q // 2
         own_cot[q].wait()
-        arrived(cot_cp[q])
+        arrived(fwd_cp[q])
 
         def step(i, carry):
             r = pl.ds(pl.multiple_of(i * 320, 320), 320)
@@ -299,6 +262,66 @@
 
     piece(0)
     piece(2)
+    a1_cp, a1_own = [], []
+    for p in range(2):
+        a1_cp.append([
+            remote(w.at[yl, c, :, (vs[p] + d) % 4, :, half(p)], a1r.at[p, vs[p]], **way(p, dv=d))
+            for d in (1, 3, 2)
+        ])
+        a1_own.append(here(w.at[yl, c, :, vs[p], :, half(p)], a1r.at[p, vs[p]]))
+    pass_on(1)
+    pass_on(3)
+    for i in range(NP):
+        pa_copy[i].wait()
+
+        def act_step(j, carry):
+            rows = pa[i % 2, pl.ds(j * 8, 8)].reshape(32, 2 * HID).astype(F32)
+            gate, up = rows[:, :HID], rows[:, HID:]
+            hid[pl.ds(pl.multiple_of(i * pt * 4 + j * 32, 32), 32), :] = (
+                gate * jax.nn.sigmoid(gate) * up
+            ).astype(BF)
+            return carry
+
+        lax.fori_loop(0, pt // 8, act_step, 0)
+        if i + 2 < NP:
+            pa_copy.append(here(pre.at[pl.ds((i + 2) * pt, pt)], pa.at[i % 2]))
+
+    actx_cp, actx_own = [], []
+    for p in range(2):
+
+        def acts_step(i, carry):
+            r = pl.ds(pl.multiple_of(i * 320, 320), 320)
+            acts[p, r, :] = dot(ohx[p, r, :], hid[:, hh(p)]).astype(BF)
+            return carry
+
+        lax.fori_loop(0, 2, acts_step, 0)
+    ahot[...] = dot(sel[...], hid[...]).astype(BF)
+    eye = onehot(iota((TOK, TOK), 0) == iota((TOK, TOK), 1))
+    aht[...] = dot(ahot[...], eye, TN).astype(BF).reshape(2, HID // 2, TOK)
+
+    def ring_part(p, d, cc):
+        return pl.ds(256 * ((c + cc) % 2) + 64 * ((us[p] + d) % 4), 64)
+
+    for p in range(2):
+        u = us[p]
+        actx_cp.append([
+            remote(acts.at[p, pl.ds(((u + d) % 4) * 160, 160)], actx.at[p, pl.ds(u * 160, 160)],
+                   **way(p, du=d))
+            for d in (1, 3, 2)
+        ])
+        actx_own.append(here(acts.at[p, pl.ds(u * 160, 160)], actx.at[p, pl.ds(u * 160, 160)]))
+    at_cp, at_own = [], []
+    for p in range(2):
+        at_cp.append([])
+        for cc in range(2):
+            for d in range(4):
+                src = aht.at[:, ring_part(p, d, cc), :]
+                dst = at.at[p, :, :, pl.ds((cc * 4 + us[p]) * TOK, TOK)]
+                if cc or d:
+                    at_cp[p].append(remote(src, dst, **way(p, du=d, dc=cc)))
+                else:
+                    at_own.append(here(src, dst))
+
     o = iota((COLD, 128), 0)
     oj = sum((o >= ROW * k).astype(jnp.int32) for k in range(1, NJ))
     orem = o - ROW * oj
@@ -317,20 +340,55 @@
             r = pl.ds(k * 4 * ROW, 4 * ROW)
             dst[r, :] = dot(px[...], src[r, :]).astype(BF)
 
-    actr_cp, actr_own = [], []
-    for p in range(2):
-        actx_own[p].wait()
-        arrived(actx_cp[p])
-
-        def actp_step(i, carry):
-            r = pl.ds(pl.multiple_of(i * 320, 320), 320)
-            actp[p, r, :] = dot(pm[r, :], actx[p]).astype(BF)
-            return carry
-
-        lax.fori_loop(0, 2, actp_step, 0)
-        a, b = spread(p, actp.at[p], actr.at[p])
-        actr_cp.append(a)
-        actr_own.append(b)
+    yr_cp = {}
+
+    def expert_hidden(n):
+        q = ORDER[n]
+        w_copy[q].wait()
+        sr_cp[q][1].wait()
+        arrived(sr_cp[q][0])
+        rows = sr.at[q]
+        if q >= 2:
+            turn(sr.at[q], sp)
+            rows = sp
+        for h in range(2):
+            for k in range(2):
+                r = pl.ds(512 * h + 256 * k, 256)
+                part = dot(rows[...], wq[q, h, k].reshape(256, DQ), NT)
+                hacc[:, r] = part if n == 0 else hacc[:, r] + part
+
+    def expert_weight(n):
+        q = ORDER[n]
+        rows = sp if q >= 2 else sr.at[q]
+        for p in range(2):
+            act = (actr.at[0], actb)[p]
+
+            def wg_step(i, carry):
+                r = pl.ds(pl.multiple_of(i * 256, 256), 256)
+                wgs[pl.ds(pl.multiple_of(p * HALFHID + i * 256, 256), 256), :] = dot(
+                    act[:, r], rows[...], TN
+                ).astype(BF)
+                return carry
+
+            lax.fori_loop(0, 2, wg_step, 0)
+        cr_cp = [
+            remote(wgs.at[pl.ds(512 * h + 256 * ((c + 1) % 2), 256)], cr.at[n % 2, h], dc=1)
+            for h in range(2)
+        ]
+
+        for cp in cr_cp:
+            cp.wait()
+        there, stay = (yl + 1) % 2, yl
+        left(sr_cp[q][0])
+        s[q, 0:256, :] = (
+            wgs[pl.ds(512 * there + 256 * c, 256), :].astype(F32)
+            + cr[n % 2, there].astype(F32)
+        ).astype(BF)
+        yr_cp[q] = remote(s.at[q, pl.ds(0, 256)], yr.at[q], dyl=1)
+        wg[:, cols(q)] = (
+            wgs[pl.ds(512 * stay + 256 * c, 256), :].astype(F32)
+            + cr[n % 2, stay].astype(F32)
+        ).astype(BF)
 
     a2_cp, a2_own, a3_cp, wh_cp, wh_own = [], [], [], [], []
     for p in range(2):
@@ -343,13 +401,26 @@
             remote(a2s.at[p, (u + d) % 4], a2r.at[p, u], **way(p, du=d)) for d in (1, 3, 2)
         ])
         a2_own.append(here(a2s.at[p, u], a2r.at[p, u]))
-    piece(1)
     for p in range(2):
         a2_own[p].wait()
         arrived(a2_cp[p])
         a3s[p] = sum(a2r[p, k].astype(F32) * hot_u[p][k] for k in range(4)).astype(BF)
         a3_cp.append(remote(a3s.at[p], a3r.at[p], dyh=1))
-    piece(3)
+    actr_cp, actr_own = [], []
+    for p in range(2):
+        actx_own[p].wait()
+        arrived(actx_cp[p])
+
+        def actp_step(i, carry):
+            r = pl.ds(pl.multiple_of(i * 320, 320), 320)
+            actp[p, r, :] = dot(pm[r, :], actx[p]).astype(BF)
+            return carry
+
+        lax.fori_loop(0, 2, actp_step, 0)
+        a, b = spread(p, actp.at[p], actr.at[p])
+        actr_cp.append(a)
+        actr_own.append(b)
+
     mine = hot_y[0] * (yh == 0).astype(F32) + hot_y[1] * (yh == 1).astype(F32)
     for p in range(2):
         arrived([a3_cp[p]])
@@ -363,6 +434,8 @@
         ])
         wh_own.append(here(ags.at[p], slot))
 
+    piece(1)
+    piece(3)
     sh = wgs
     diag = iota((TOK, TOK), 0) == iota((TOK, TOK), 1)
     hh_cp, hh_own, rs_cp, rs_own = [], [], [], []
@@ -384,8 +457,14 @@
                 sh[pl.ds(b * TOK, TOK), :] = (block.astype(F32) * col).astype(BF)
             hp[q] = dot(at[p].reshape(128, 8 * TOK), sh[...]).astype(BF)
             part = dot(wh[p, :, :, :, pl.ds(i * DQ, DQ)].reshape(128, DQ), sh[...], NT)
-            hacc[0:128, :] = part if i == 0 else hacc[0:128, :] + part
-        hhs[p] = hacc[0:128, :].astype(BF).reshape(2, 64, 8 * TOK)
+            for k in range(8):
+                t, r = pl.ds(k * 128, 128), pl.ds((k % 4) * 128, 128)
+                if i == 0:
+                    gc[k // 4, r, :] = part[:, k * 128:(k + 1) * 128]
+                else:
+                    hhs[p, :, :, t] = (
+                        gc[k // 4, r, :] + part[:, k * 128:(k + 1) * 128]
+                    ).astype(BF).reshape(2, 64, TOK)
         hh_cp.append([])
         for cc in range(2):
             for d in range(4):
@@ -416,52 +495,12 @@
         actr_own[p].wait()
         arrived(actr_cp[p])
     turn(actr.at[1], actb)
-    yr_cp = {}
-    last_ys = {}
-    for n, q in enumerate(ORDER):
-        w_copy[q].wait()
-        sr_cp[q][1].wait()
-        arrived(sr_cp[q][0])
-        rows = sr.at[q]
-        if q >= 2:
-            turn(sr.at[q], sp)
-            rows = sp
-
-        for p in range(2):
-            act = (actr.at[0], actb)[p]
-
-            def wg_step(i, carry):
-                r = pl.ds(pl.multiple_of(i * 256, 256), 256)
-                wgs[pl.ds(pl.multiple_of(p * HALFHID + i * 256, 256), 256), :] = dot(
-                    act[:, r], rows[...], TN
-                ).astype(BF)
-                return carry
-
-            lax.fori_loop(0, 2, wg_step, 0)
-        cr_cp = [
-            remote(wgs.at[pl.ds(512 * h + 256 * ((c + 1) % 2), 256)], cr.at[n % 2, h], dc=1)
-            for h in range(2)
-        ]
-
-        for h in range(2):
-            for k in range(2):
-                r = pl.ds(512 * h + 256 * k, 256)
-                part = dot(rows[...], wq[q, h, k].reshape(256, DQ), NT)
-                hacc[:, r] = part if n == 0 else hacc[:, r] + part
-        for cp in cr_cp:
-            cp.wait()
-        there, stay = (yl + 1) % 2, yl
-        if n >= 2:
-            yr_cp[ORDER[n - 2]].wait_send()
-        ys[n % 2] = (
-            wgs[pl.ds(512 * there + 256 * c, 256), :].astype(F32)
-            + cr[n % 2, there].astype(F32)
-        ).astype(BF)
-        yr_cp[q] = remote(ys.at[n % 2], yr.at[q], dyl=1)
-        wg[:, cols(q)] = (
-            wgs[pl.ds(512 * stay + 256 * c, 256), :].astype(F32)
-            + cr[n % 2, stay].astype(F32)
-        ).astype(BF)
+    for n in range(2):
+        expert_hidden(n)
+        expert_weight(n)
+
+    expert_hidden(2)
+    expert_hidden(3)
     for p in range(2):
         left(actx_cp[p])
     hg = acts
@@ -484,6 +523,19 @@
         gp[p] = sum(rsb[p, k].astype(F32) for k in range(16)).astype(BF)
         g1_cp.append([remote(gp.at[p], g1.at[p, vs[p]], **way(p, dv=d)) for d in (1, 3, 2)])
         g1_own.append(here(gp.at[p], g1.at[p, vs[p]]))
+
+    for p in range(2):
+        g1_own[p].wait()
+        arrived(g1_cp[p])
+        g2_cp.append(remote(g1.at[p], g2.at[p, yh], dyh=1))
+        g2_own.append(here(g1.at[p], g2.at[p, yh]))
+    expert_weight(2)
+    for p in range(2):
+        g2_own[p].wait()
+        arrived([g2_cp[p]])
+        g3_cp.append([remote(g2.at[p], g3.at[p, us[p]], **way(p, du=d)) for d in (1, 3, 2)])
+        g3_own.append(here(g2.at[p], g3.at[p, us[p]]))
+    expert_weight(3)
 
     hgp = actp
     ret_cp, ret_own = [], []
@@ -503,22 +555,16 @@
         ret_own.append(here(hgp.at[p, pl.ds(u * 160, 160)], ret.at[p, pl.ds(u * 160, 160)]))
 
     for p in range(2):
-        g1_own[p].wait()
-        arrived(g1_cp[p])
-        g2_cp.append(remote(g1.at[p], g2.at[p, yh], dyh=1))
-        g2_own.append(here(g1.at[p], g2.at[p, yh]))
-    for p in range(2):
         hh_own[p].wait()
         arrived(hh_cp[p])
     ahot[...] = (
         dot(eye, hht[0].reshape(HID, TOK), NT) + dot(eye, hht[1].reshape(HID, TOK), NT)
     ).astype(BF)
-    for p in range(2):
-        g2_own[p].wait()
-        arrived([g2_cp[p]])
-        g3_cp.append([remote(g2.at[p], g3.at[p, us[p]], **way(p, du=d)) for d in (1, 3, 2)])
-        g3_own.append(here(g2.at[p], g3.at[p, us[p]]))
-
+
+    for n, q in enumerate(ORDER):
+        yr_cp[q].wait_recv()
+        sent.append(yr_cp[q])
+        wg[:, cols(q)] = (wg[:, cols(q)].astype(F32) + yr[q].astype(F32)).astype(BF)
     for p in range(2):
         ret_own[p].wait()
         arrived(ret_cp[p])
@@ -526,11 +572,6 @@
             r, t = pl.ds(i * 256, 256), pl.ds(p * HALFHID + i * 256, 256)
             hid[:, t] = (dot(ohx[p], ret[p, :, r], TN) + dot(sel[...], ahot[:, t], TN)).astype(BF)
 
-    for n, q in enumerate(ORDER):
-        yr_cp[q].wait_recv()
-        if n >= 2:
-            sent.append(yr_cp[q])
-        wg[:, cols(q)] = (wg[:, cols(q)].astype(F32) + yr[q].astype(F32)).astype(BF)
     own = (e1 == e).astype(F32)
     is_hot = jnp.sum(own * hotv, axis=0, keepdims=True)
     for p in range(2):
@@ -552,10 +593,11 @@
     return pltpu.VMEM(shape, dtype)
 
 
-def run_main(cot, meta, rnat, pre, w):
+def run_main(cot, rt, gt, pre, w):
     anyw = pl.BlockSpec(memory_space=pl.ANY)
     vmem = pl.BlockSpec(memory_space=pltpu.VMEM)
     scratch = [
+        vm(8, 128, dtype=F32),
         vm(NQ, SLOT, DQ), vm(NQ, SLOT, DQ), vm(2, 8, 8, 128, dtype=F32),
         vm(2, TOK // 4, TOPK, 2 * HID), vm(NQ, 2, 2, 4, 4, 16, DQ),
         vm(2, COLD, SLOT), vm(TOK, SLOT), vm(2, COLD, SLOT), vm(COLD, COLD),
@@ -564,7 +606,7 @@
         vm(COLD, HALFHID),
         vm(NQ, COLD, DQ), vm(NQ, COLD, DQ), vm(COLD, DQ), vm(COLD, HID, dtype=F32),
         vm(2, COLD, HALFHID), vm(2, COLD, HALFHID),
-        vm(HID, DQ), vm(2, 2, 256, DQ), vm(2, 256, DQ), vm(NQ, 256, DQ),
+        vm(HID, DQ), vm(2, 2, 256, DQ), vm(NQ, 256, DQ),
         vm(2, 4, 4, 16, HALF), vm(2, 4, 16, HALF), vm(2, 4, 16, HALF),
         vm(2, 16, HALF), vm(2, 16, HALF), vm(2, 16, HALF), vm(2, 2, 4, 16, HALF),
         vm(TOK, HID), vm(2, HID // 2, TOK), vm(2, 2, 64, 8 * TOK), vm(2, 2, HID // 2, TOK),
@@ -589,7 +631,7 @@
         cost_estimate=pl.CostEstimate(
             flops=22 * 10**9, bytes_accessed=16 * 10**6, transcendentals=10**6
         ),
-    )(cot, meta, rnat, pre, w)
+    )(cot, rt, gt, pre, w)
 
 
 def grad_kernel(h, p, o):
@@ -620,10 +662,8 @@
 
 
 def local(cotangent, routes, gates, pre_act, down_weight):
-    meta = jnp.concatenate([routes.astype(F32).T, gates.T], axis=0)
-    rnat = routes.astype(F32).reshape(1, SLOT)
     hidden, weight = run_main(
-        cotangent, meta, rnat, pre_act, down_weight.reshape(2, 2, 4, 4, 16, D)
+        cotangent, routes.T, gates.T, pre_act, down_weight.reshape(2, 2, 4, 4, 16, D)
     )
     return run_grad(hidden, pre_act), weight[None]
 

time: 179 us -> 168 us (0.939)
  Pallas kernels: 173 us -> 165 us
  other arithmetic: 1.96 us -> 0 us
    pallas_call x1, Pallas kernels: 170 us -> 161 us  [run_main(): pl.pallas_call(main_kernel, out_shape=(jax.ShapeDtypeStruct((SLOT, HID),...]
where the time goes in v3:
time: 168 us
  Pallas kernels  165 us (98%)
  local copies, waits for them, and re-layouts  2.45 us (1%)
    pallas_call x1, Pallas kernels, run_main(): pl.pallas_call(main_kernel, out_shape=(jax.ShapeDtypeStruct((SLOT, HID),...  161 us
    pallas_call x1, Pallas kernels, run_grad(): pl.pallas_call(grad_kernel, grid=(TOK // n,), out_shape=jax.ShapeDtypeStr...  3.74 us

profile of v3, /device:TPU:1, one launch (start us, length us, event | category | flops | bytes accessed | tf_op | source)
XLA Modules:
  0.0 167.9 jit_solution(14763739573887509465)
XLA Ops:
  0.6 0.0 copy-start
  0.6 161.0 %shard_map.68 = (bf16[512,1024]{1,0:T(8,128)(2,1)}, bf16[256,3584]{1,0:T(8,128)(2,1)}) custom-call(bf16[128,3584]{1,0:T(8,128)(2,1)} %cot.1, s32[4,128]{1,0:T(4,128)} %bitcast.6, f32[4,128]{1,0:T(4,128)} %bitcast.7, bf16[128,4,2048]{2,1,0:T(4,128)(2,1)} %p.1, bf16[2,2,4,4,16,3584]{5,4,3,2,1,0:T(8,128)(2,1)} %bitcast.5), custom_call_target="tpu_custom_call" | custom-call | flops 22000001024 | bytes 16000000 | tf_op jit(solution)/shard_map/pallas_call | solution.py:619
  161.7 0.0 copy-done
  161.7 0.0 copy-start.1
  161.7 1.2 copy-done.1
  162.9 0.0 copy-start.2
  162.9 3.7 %shard_map.69 = bf16[128,4,2048]{2,1,0:T(4,128)(2,1)} custom-call(bf16[512,1024]{1,0:T(8,128)(2,1)S(1)} %copy-done.1, bf16[128,4,2048]{2,1,0:T(4,128)(2,1)S(1)} %copy-done), custom_call_target="tpu_custom_call" | custom-call | tf_op jit(solution)/shard_map/pallas_call | solution.py:651
  166.7 0.0 copy-done.2
  166.7 1.2 copy.8
Async XLA Ops:
  0.6 161.1 %copy-start = (bf16[128,4,2048]{2,1,0:T(4,128)(2,1)S(1)}, bf16[128,4,2048]{2,1,0:T(4,128)(2,1)}, u32[]{:S(2)}) copy-start(bf16[128,4,2048]{2,1,0:T(4,128)(2,1)} %p.1) | copy-start | bytes 6291460
  161.7 1.2 copy-start.1
  162.9 3.7 %copy-start.2 = (bf16[256,3584]{1,0:T(8,128)(2,1)S(1)}, bf16[256,3584]{1,0:T(8,128)(2,1)}, u32[]{:S(2)}) copy-start(bf16[256,3584]{1,0:T(8,128)(2,1)} %get-tuple-element.5) | copy-start | bytes 5505028

commit v4 on v3

--- a/solution.py
+++ b/solution.py
@@ -647,7 +647,7 @@
 
 
 def run_grad(hidden, pre):
-    n = 16
+    n = 32
     return pl.pallas_call(
         grad_kernel,
         grid=(TOK // n,),

time: 168 us -> 167 us (level)
  no operation moved by 1% of the time
where the time goes in v4:
time: 167 us
  Pallas kernels  164 us (98%)
  local copies, waits for them, and re-layouts  2.45 us (1%)
    pallas_call x1, Pallas kernels, run_main(): pl.pallas_call(main_kernel, out_shape=(jax.ShapeDtypeStruct((SLOT, HID),...  161 us

profile of v4, /device:TPU:1, one launch (start us, length us, event | category | flops | bytes accessed | tf_op | source)
XLA Modules:
  0.0 166.9 jit_solution(13604925055607402658)
XLA Ops:
  0.6 0.0 copy-start
  0.6 161.0 %shard_map.68 = (bf16[512,1024]{1,0:T(8,128)(2,1)}, bf16[256,3584]{1,0:T(8,128)(2,1)}) custom-call(bf16[128,3584]{1,0:T(8,128)(2,1)} %cot.1, s32[4,128]{1,0:T(4,128)} %bitcast.6, f32[4,128]{1,0:T(4,128)} %bitcast.7, bf16[128,4,2048]{2,1,0:T(4,128)(2,1)} %p.1, bf16[2,2,4,4,16,3584]{5,4,3,2,1,0:T(8,128)(2,1)} %bitcast.5), custom_call_target="tpu_custom_call" | custom-call | flops 22000001024 | bytes 16000000 | tf_op jit(solution)/shard_map/pallas_call | solution.py:619
  161.7 0.0 copy-done
  161.7 0.0 copy-start.1
  161.7 1.2 copy-done.1
  162.9 0.0 copy-start.2
  162.9 2.7 %shard_map.69 = bf16[128,4,2048]{2,1,0:T(4,128)(2,1)} custom-call(bf16[512,1024]{1,0:T(8,128)(2,1)S(1)} %copy-done.1, bf16[128,4,2048]{2,1,0:T(4,128)(2,1)S(1)} %copy-done), custom_call_target="tpu_custom_call" | custom-call | tf_op jit(solution)/shard_map/pallas_call | solution.py:651
  165.6 0.0 copy-done.2
  165.6 1.2 copy.8
Async XLA Ops:
  0.6 161.1 %copy-start = (bf16[128,4,2048]{2,1,0:T(4,128)(2,1)S(1)}, bf16[128,4,2048]{2,1,0:T(4,128)(2,1)}, u32[]{:S(2)}) copy-start(bf16[128,4,2048]{2,1,0:T(4,128)(2,1)} %p.1) | copy-start | bytes 6291460
  161.7 1.2 copy-start.1
  162.9 2.7 %copy-start.2 = (bf16[256,3584]{1,0:T(8,128)(2,1)S(1)}, bf16[256,3584]{1,0:T(8,128)(2,1)}, u32[]{:S(2)}) copy-start(bf16[256,3584]{1,0:T(8,128)(2,1)} %get-tuple-element.5) | copy-start | bytes 5505028
